TPU v7x, 32 devices: a whole 2x2x4 slice. The times are simulated.
32 devices in a mesh: dp: 2 (over x), seq: 4 (over y, core), heads: 4 (over z).
Axes of the slice: x: 2, y: 2, z: 4, core: 2. Of those that a mesh axis runs over, the one named last changes fastest.
Arguments:
- tokens: bfloat16 [8, 1024, 1024], P('dp', ('seq', 'heads')), may hold values from -6 to 6
- querymap: bfloat16 [1024, 1024], P(None, 'heads'), may hold values from -0.1875 to 0.1875
- querybias: bfloat16 [1024], P('heads'), may hold values from -2 to 2
- keymap: bfloat16 [1024, 1024], P(None, 'heads'), may hold values from -0.1875 to 0.1875
- valuemap: bfloat16 [1024, 1024], P(None, 'heads'), may hold values from -0.1875 to 0.1875
- valuebias: bfloat16 [1024], P('heads'), may hold values from -2 to 2
- mergemap: bfloat16 [1024, 1024], P('heads'), may hold values from -0.5 to 0.5
- mergebias: bfloat16 [1024], replicated, may hold values from -2 to 2
- normgain: bfloat16 [1024], replicated, may hold values from 0.69921875 to 1.296875
- normshift: bfloat16 [1024], replicated, may hold values from -2 to 2
- innermap: bfloat16 [1024, 4096], P(None, 'heads'), may hold values from -0.1875 to 0.1875
- innerbias: bfloat16 [4096], P('heads'), may hold values from -2 to 2
- outermap: bfloat16 [4096, 1024], P('heads'), may hold values from -0.09375 to 0.09375
- outerbias: bfloat16 [1024], replicated, may hold values from -2 to 2
- finalgain: bfloat16 [1024], replicated, may hold values from 0.69921875 to 1.296875
- finalshift: bfloat16 [1024], replicated, may hold values from -2 to 2
- lengths: int32 [8], P('dp'), may hold values from 16 to 1024, as said below
- cotangent: bfloat16 [8, 1024, 1024], P('dp', ('seq', 'heads')), may hold values from -6 to 6
Outputs:
- layer_output: bfloat16 [8, 1024, 1024], P('dp', ('seq', 'heads'))
- tokens_grad: bfloat16 [8, 1024, 1024], P('dp', ('seq', 'heads'))
- querymap_grad: float32 [1024, 1024], P(None, 'heads')
- querybias_grad: float32 [1024], P('heads')
- keymap_grad: float32 [1024, 1024], P(None, 'heads')
- valuemap_grad: float32 [1024, 1024], P(None, 'heads')
- valuebias_grad: float32 [1024], P('heads')
- mergemap_grad: float32 [1024, 1024], P('heads')
- mergebias_grad: float32 [1024], replicated
- normgain_grad: float32 [1024], replicated
- normshift_grad: float32 [1024], replicated
- innermap_grad: float32 [1024, 4096], P(None, 'heads')
- innerbias_grad: float32 [4096], P('heads')
- outermap_grad: float32 [4096, 1024], P('heads')
- outerbias_grad: float32 [1024], replicated
- finalgain_grad: float32 [1024], replicated
- finalshift_grad: float32 [1024], replicated
Inputs may be any that keep to these rules, and one draw needn't show every extreme that they name: `lengths`: in each aligned block of 4 proteins (those of one dp index) one protein, drawn from the seed, has length 1024; the others are mostly short.
All inputs are finite; a program needn't handle non-finite values.
Results may differ from a plain program's by a relative error of at most 0.02.
Values may be sent and summed in bfloat16 or wider, within the bound.
No kernel may reach another device: no remote copies, remote signals or barrier semaphores. Data moves between devices by JAX's collectives and lax.ppermute only.
A program may use at most 192 MiB of HBM per device.

v0:
```python
import functools

import jax
import jax.numpy as jnp
from jax import lax
from jax.experimental import pallas as pl
from jax.experimental.pallas import tpu as pltpu
from jax.sharding import PartitionSpec as P

HEAD_DIM = 64


epsilon = 1e-06
score_scale = 0.125
masked_score = -1000000000.0
low = jnp.bfloat16
wide = jnp.float32
vmem_bytes = 48 * 1024 * 1024


def dot(a, b):
    return jnp.dot(a, b, preferred_element_type=wide)


def dot_nt(a, b):
    return lax.dot_general(a, b, (((1,), (1,)), ((), ())), preferred_element_type=wide)


def dot_tn(a, b):
    return lax.dot_general(a, b, (((0,), (0,)), ((), ())), preferred_element_type=wide)


def swap(value, axis, stride):
    size = lax.axis_size(axis)
    return lax.ppermute(value, axis, [(i, i ^ stride) for i in range(size)])


def swap_slots(value, mask):
    size = lax.axis_size("dp") * lax.axis_size("seq")
    return lax.ppermute(value, ("dp", "seq"), [(i, i ^ mask) for i in range(size)])


def bit_of(bit):
    axis, stride = bit
    return (lax.axis_index(axis) // stride) % 2


def add_low(a, b):
    return (a.astype(wide) + b.astype(wide)).astype(low)


def params(mebibytes):
    return pltpu.CompilerParams(vmem_limit_bytes=mebibytes * 1024 * 1024)


in_vmem = pl.BlockSpec(memory_space=pltpu.VMEM)
in_smem = pl.BlockSpec(memory_space=pltpu.SMEM)
anywhere = pl.BlockSpec(memory_space=pl.ANY)
in_hbm = pl.BlockSpec(memory_space=pltpu.HBM)
hbm = True
kernels_alone = ("attend", "attend_back", "merge_norm", "project", "join_units", "stack_pairs")


def kernel_call(
    body, name, arrays, out, scalars=(), scratch=(), mebibytes=16, waits=(), far_in=(), local=(), flops=1
):
    ns, na, nw, no, nl = len(scalars), len(arrays), len(waits), len(out), len(local)
    alone = name in kernels_alone
    far_in = [i for i in range(na) if alone and (far_in is hbm or i in far_in)]
    far_out = [i for i, o in enumerate(out) if alone and len(o) > 2 and o[2] is hbm]
    own_out = [i for i, o in enumerate(out) if len(o) > 2 and o[2] == "kernel"]
    buffers = [pltpu.VMEM(arrays[i].shape, arrays[i].dtype) for i in far_in]
    buffers += [pltpu.VMEM(out[i][0], out[i][1]) for i in far_out]
    count = len(buffers)

    def whole(*refs):
        here = list(refs[: ns + na])
        at = ns + na + nw
        kept, outs, rest = refs[at : at + nl], list(refs[at + nl : at + nl + no]), refs[at + nl + no :]
        rest, (*held_refs, sems) = (rest[: len(rest) - count - 1], rest[len(rest) - count - 1 :])
        copies = []
        for k, i in enumerate(far_in):
            copies.append(pltpu.make_async_copy(here[ns + i], held_refs[k], sems.at[k]))
            copies[-1].start()
            here[ns + i] = held_refs[k]
        for copy in copies:
            copy.wait()
        copies = []
        for k, i in enumerate(far_out, len(far_in)):
            copies.append(pltpu.make_async_copy(held_refs[k], outs[i], sems.at[k]))
            outs[i] = held_refs[k]
        body(*here, *kept, *outs, *rest)
        for copy in copies:
            copy.start()
        for copy in copies:
            copy.wait()

    return pl.pallas_call(
        whole,
        in_specs=[in_smem] * ns
        + [in_hbm if i in far_in else in_vmem for i in range(na)]
        + [anywhere] * nw
        + [in_hbm] * nl,
        out_specs=[in_hbm if i in far_out + own_out else in_vmem for i in range(no)],
        out_shape=[jax.ShapeDtypeStruct(o[0], o[1]) for o in out],
        scratch_shapes=list(scratch) + buffers + [pltpu.SemaphoreType.DMA((max(count, 1),))],
        compiler_params=params(60 if alone else mebibytes),
        cost_estimate=pl.CostEstimate(flops=flops, bytes_accessed=1, transcendentals=0),
        name=name,
    )(*scalars, *arrays, *waits, *local)


def nothing(*refs):
    pass


def gate(values, waits):
    values = [pltpu.with_memory_space_constraint(v, pltpu.HBM) for v in values]
    found = pl.pallas_call(
        nothing,
        in_specs=[anywhere] * (len(values) + len(waits)),
        out_specs=[anywhere] * len(values),
        out_shape=[jax.ShapeDtypeStruct(v.shape, v.dtype) for v in values],
        input_output_aliases={i: i for i in range(len(values))},
        compiler_params=params(1),
        name="gate",
    )(*values, *waits)
    return list(found)


def pad16(count):
    return -(-count // 16) * 16


def place(pos, proteins, groups, share, i, j):
    seq, heads = pos[proteins], pos[proteins + 1]
    return pl.multiple_of(((seq ^ i) * groups + (heads ^ j)) * share, share)


def masked(scores, length, first):
    key_at = first + lax.broadcasted_iota(jnp.int32, scores.shape, 0)
    return jnp.where(key_at < length, scores, masked_score)


def chunks(n, block):
    return [(0, n - block, False)] * (n > block) + [(n - block, n, True)]


def piece_list(refs, groups):
    found, count = [], 0
    for ref in refs:
        for n in range(ref.shape[0]):
            found.append((ref, count // groups, count % groups, n))
            count += 1
    return found


def start_keys(pos, p, proteins, groups, kv_refs, kv_all, sems, blocks, block, wait):
    share = kv_refs[0].shape[2]
    for k, (ref, i, j, n) in enumerate(piece_list(kv_refs, groups)):
        at = place(pos, proteins, groups, share, i, j)

        @pl.when(at < blocks * block)
        def _():
            copy = pltpu.make_async_copy(ref.at[n, p], kv_all.at[p, pl.ds(at, share), :], sems.at[p])
            if wait:
                copy.wait()
            else:
                copy.start()


def query_rows(refs, p):
    found = [ref[n, p] for ref in refs for n in range(ref.shape[0])]
    return jnp.concatenate(found) * jnp.asarray(score_scale, low)


def attend_kernel(counts, pos, *refs):
    stacks, arrays, groups = counts
    q_refs, kv_refs = refs[:stacks], refs[stacks : stacks + arrays]
    ctx_refs, (ctx_t_ref, lse_ref, kv_all, sems) = refs[stacks + arrays : -4], refs[-4:]
    _, proteins, share, width = q_refs[0].shape
    total = kv_all.shape[1]
    block = min(256, total)
    heads = range(width // HEAD_DIM)

    def keys_of(p, wait):
        blocks = (pos[p] + block - 1) // block
        start_keys(pos, p, proteins, groups, kv_refs, kv_all, sems, blocks, block, wait)
        return blocks

    for p in range(proteins):
        keys_of(p, False)

    def protein(p, carry):
        length = pos[p]
        blocks = keys_of(p, True)

        def body(count):
            n = count * block
            queries = query_rows(q_refs, p)
            cols = lambda h: slice(h * HEAD_DIM, (h + 1) * HEAD_DIM)
            value_cols = lambda h: slice(width + h * HEAD_DIM, width + (h + 1) * HEAD_DIM)
            cuts = chunks(n, block)
            scores = [
                [dot_nt(kv_all[p, a:b, cols(h)], queries[:, cols(h)]) for a, b, _ in cuts]
                for h in heads
            ]
            weights, denominators = [], []
            for h in heads:
                found = [
                    masked(value, length, a) if last else value
                    for value, (a, _, last) in zip(scores[h], cuts)
                ]
                high = functools.reduce(
                    jnp.maximum, [jnp.max(value, axis=0, keepdims=True) for value in found]
                )
                found = [jnp.exp(value - high) for value in found]
                denominator = sum(jnp.sum(value, axis=0, keepdims=True) for value in found)
                lse_ref[p, h : h + 1, :] = high + jnp.log(denominator)
                weights.append([value.astype(low) for value in found])
                denominators.append(denominator)
            context_t = jnp.concatenate(
                [
                    sum(
                        dot_tn(kv_all[p, a:b, value_cols(h)], value)
                        for (a, b, _), value in zip(cuts, weights[h])
                    )
                    / denominators[h]
                    for h in heads
                ]
            )
            ctx_t_ref[p] = context_t
            context = context_t.T.astype(low)
            for j, ref in enumerate(ctx_refs):
                ref[p] = context[j * share : (j + 1) * share]

        for count in range(1, total // block + 1):
            pl.when(blocks == count)(functools.partial(body, count))
        return carry

    lax.fori_loop(0, proteins, protein, 0)


def attend_back_kernel(counts, pos, *refs):
    stacks, arrays, groups = counts
    q_refs, dctx_refs, refs = refs[:stacks], refs[stacks : stacks + groups], refs[stacks + groups :]
    ctx_t_ref, lse_ref, kv_refs, refs = refs[0], refs[1], refs[2 : 2 + arrays], refs[2 + arrays :]
    dq_ref, dkv_refs, (kv_all, dkv_all, dq_all, sems, out_sems) = refs[0], refs[1:-5], refs[-5:]
    _, proteins, share, width = q_refs[0].shape
    rows = groups * share
    total = kv_all.shape[1]
    block = min(256, total)
    heads = range(width // HEAD_DIM)

    def keys_of(p, wait):
        blocks = jnp.where(pos[proteins] * rows < pos[p], (pos[p] + block - 1) // block, 0)
        start_keys(pos, p, proteins, groups, kv_refs, kv_all, sems, blocks, block, wait)
        return blocks

    for p in range(proteins):
        keys_of(p, False)

    def results_of(p, wait):
        for j in range(groups):
            copy = pltpu.make_async_copy(
                dq_all.at[p, pl.ds(j * share, share), :], dq_ref.at[j, p], out_sems.at[p]
            )
            copy.wait() if wait else copy.start()
            for i, ref in enumerate(dkv_refs):
                at = place(pos, proteins, groups, share, i, j)
                copy = pltpu.make_async_copy(
                    dkv_all.at[p, pl.ds(at, share), :], ref.at[j, p], out_sems.at[p]
                )
                copy.wait() if wait else copy.start()

    def protein(p, carry):
        length = pos[p]
        blocks = keys_of(p, True)

        @pl.when(blocks == 0)
        def _():
            dkv_all[p] = jnp.zeros(dkv_all.shape[1:], low)
            dq_all[p] = jnp.zeros(dq_all.shape[1:], low)

        def body(count):
            n = count * block
            queries = query_rows(q_refs, p)
            dctx = jnp.concatenate([ref[p] for ref in dctx_refs])
            product = dctx.astype(wide).T * ctx_t_ref[p]
            cols = lambda h: slice(h * HEAD_DIM, (h + 1) * HEAD_DIM)
            value_cols = lambda h: slice(width + h * HEAD_DIM, width + (h + 1) * HEAD_DIM)
            deltas = [jnp.sum(product[cols(h), :], axis=0, keepdims=True) for h in heads]
            dq = []
            for a, b, last in chunks(n, block):
                scores = [dot_nt(kv_all[p, a:b, cols(h)], queries[:, cols(h)]) for h in heads]
                dprobs = [dot_nt(kv_all[p, a:b, value_cols(h)], dctx[:, cols(h)]) for h in heads]
                probs, dscores = [], []
                for h in heads:
                    score = masked(scores[h], length, a) if last else scores[h]
                    prob = jnp.exp(score - lse_ref[p, h : h + 1, :])
                    probs.append(prob.astype(low))
                    dscores.append((prob * (dprobs[h] - deltas[h])).astype(low))
                dv = [dot(probs[h], dctx[:, cols(h)]) for h in heads]
                dk = [dot(dscores[h], queries[:, cols(h)]) for h in heads]
                dq.append(
                    jnp.concatenate([dot_tn(kv_all[p, a:b, cols(h)], dscores[h]) for h in heads])
                )
                dkv_all[p, a:b, :width] = jnp.concatenate(dk, axis=1).astype(low)
                dkv_all[p, a:b, width:] = jnp.concatenate(dv, axis=1).astype(low)
            if n < total:
                dkv_all[p, n:, :] = jnp.zeros((total - n, 2 * width), low)
            dq_all[p] = (sum(dq).T * score_scale).astype(low)

        for count in range(1, total // block + 1):
            pl.when(blocks == count)(functools.partial(body, count))
        results_of(p, False)
        return carry

    lax.fori_loop(0, proteins, protein, 0)
    for p in range(proteins):
        results_of(p, True)


def attend(pos, queries, kv_pieces, waits):
    groups = sum(q.shape[0] for q in queries)
    _, proteins, share, width = queries[0].shape
    rows = groups * share
    total = share * sum(piece.shape[0] for piece in kv_pieces)
    found = kernel_call(
        functools.partial(attend_kernel, (len(queries), len(kv_pieces), groups)),
        "attend",
        queries,
        [((proteins, share, width), low, hbm)] * groups
        + [((proteins, width, rows), wide, hbm), ((proteins, 8, rows), wide, hbm)],
        scalars=[pos],
        scratch=[
            pltpu.VMEM((proteins, total, 2 * width), low),
            pltpu.SemaphoreType.DMA((proteins,)),
        ],
        mebibytes=32,
        far_in=hbm,
        local=kv_pieces,
        waits=waits,
        flops=int(1e10),
    )
    return found[:groups], found[groups], found[groups + 1]


def attend_back(pos, queries, dctx, ctx_t, lse, kv_pieces, waits):
    groups = len(dctx)
    _, proteins, share, width = queries[0].shape
    total = share * sum(piece.shape[0] for piece in kv_pieces)
    pieces = total // (groups * share)
    arrays = [*queries, *dctx, ctx_t, lse]
    found = kernel_call(
        functools.partial(attend_back_kernel, (len(queries), len(kv_pieces), groups)),
        "attend_back",
        arrays,
        [((groups, proteins, share, width), low, "kernel")]
        + [((groups, proteins, share, 2 * width), low, "kernel")] * pieces,
        scalars=[pos],
        scratch=[
            pltpu.VMEM((proteins, total, 2 * width), low),
            pltpu.VMEM((proteins, total, 2 * width), low),
            pltpu.VMEM((proteins, groups * share, width), low),
            pltpu.SemaphoreType.DMA((proteins,)),
            pltpu.SemaphoreType.DMA((proteins,)),
        ],
        mebibytes=32,
        far_in=[i for i in range(len(arrays)) if not 0 <= i - len(queries) < groups],
        local=kv_pieces,
        waits=waits,
        flops=int(2e10),
    )
    return found[0], found[1:]


def project_kernel(count, *refs):
    tok_refs, (qmap_ref, kmap_ref, vmap_ref, qbias_ref, vbias_ref, q_ref, kv_ref) = refs[:count], refs[count:]
    width = q_ref.shape[-1]
    for j, tok_ref in enumerate(tok_refs):
        shape = q_ref.shape[1:]
        queries = dot(tok_ref[...], qmap_ref[...]) + qbias_ref[...].astype(wide)
        q_ref[j] = queries.astype(low).reshape(shape)
        kv_ref[j, :, :, :width] = dot(tok_ref[...], kmap_ref[...]).astype(low).reshape(shape)
        values = dot(tok_ref[...], vmap_ref[...]) + vbias_ref[...].astype(wide)
        kv_ref[j, :, :, width:] = values.astype(low).reshape(shape)


def project(tok, maps, proteins, waits=()):
    width = maps[0].shape[1]
    share = tok[0].shape[0] // proteins
    return kernel_call(
        functools.partial(project_kernel, len(tok)),
        "project",
        [*tok, *maps],
        [
            ((len(tok), proteins, share, width), low, hbm),
            ((len(tok), proteins, share, 2 * width), low, hbm),
        ],
        waits=waits,
        far_in=hbm,
    )


def unit_of(values):
    centered = values - jnp.mean(values, axis=-1, keepdims=True)
    variance = jnp.mean(centered * centered, axis=-1, keepdims=True)
    inverse = lax.rsqrt(variance + epsilon)
    return centered * inverse, inverse


def norm_back(grad_rows, unitized, inverse, scales):
    scaled = grad_rows * scales
    grad_mean = jnp.mean(scaled, axis=-1, keepdims=True)
    cross_mean = jnp.mean(scaled * unitized, axis=-1, keepdims=True)
    return inverse * (scaled - grad_mean - unitized * cross_mean)


def steps(rows):
    size = 64 if rows % 64 == 0 else rows
    return [slice(at, at + size) for at in range(0, rows, size)]


def merge_kernel(groups, heads, *refs):
    ctx_refs, refs = refs[:groups], refs[groups:]
    own_map, maps_all, tok_ref, small_ref = refs[:4]
    normed_ref, low_ref, unit_ref, inv_ref, maps_ref = refs[4:]
    others = groups - 1
    slots, _, size, _ = maps_all.shape
    for j in range(others):
        for k in range(slots):
            maps_ref[j, k * size : (k + 1) * size, :] = maps_all[k, heads[0] ^ (j + 1)]
    merged = small_ref[0:1, :] + dot(ctx_refs[0][...], own_map[...])
    for j in range(others):
        merged += dot(ctx_refs[j + 1][...], maps_ref[j])
    unit_ref[...] = tok_ref[...].astype(wide) + merged
    for rows in steps(tok_ref.shape[0]):
        unit, inverse = unit_of(unit_ref[rows, :])
        normed = unit * small_ref[1:2, :] + small_ref[2:3, :]
        normed_ref[rows, :] = normed
        low_ref[rows, :] = normed.astype(low)
        unit_ref[rows, :] = unit
        inv_ref[rows, :] = jnp.broadcast_to(inverse, (inverse.shape[0], 128))


def merge_norm(heads, ctx, own_map, maps_all, tok, small, waits):
    rows, model = tok.shape
    groups = len(ctx)
    return kernel_call(
        functools.partial(merge_kernel, groups),
        "merge_norm",
        [*ctx, own_map, maps_all, tok, small],
        [
            ((rows, model), wide, hbm),
            ((rows, model), low, hbm),
            ((rows, model), wide, hbm),
            ((rows, 128), wide, hbm),
            ((groups - 1, *own_map.shape), low, hbm),
        ],
        scalars=[heads],
        waits=waits,
        far_in=hbm,
    )


def final_kernel(*refs):
    normed_ref, near_ref, core_ref, far_ref, small_ref, cot_ref, live_ref = refs[:7]
    out_ref, dsum_ref, dbranch_ref, sums_ref = refs[7:]
    gain = small_ref[4:5, :]
    gain_sum = shift_sum = bias_sum = 0.0
    for rows in steps(normed_ref.shape[0]):
        branch = near_ref[rows, :].astype(wide) + core_ref[rows, :].astype(wide)
        branch = branch + far_ref[rows, :].astype(wide) + small_ref[3:4, :]
        unit, inverse = unit_of(normed_ref[rows, :] + branch)
        out_ref[rows, :] = (unit * gain + small_ref[5:6, :]).astype(low)
        grad = cot_ref[rows, :].astype(wide) * live_ref[rows, 0:1]
        dsum = norm_back(grad, unit, inverse, gain)
        dsum_ref[rows, :] = dsum
        dbranch = dsum.astype(low)
        dbranch_ref[rows, :] = dbranch
        gain_sum += jnp.sum(grad * unit, axis=0, keepdims=True)
        shift_sum += jnp.sum(grad, axis=0, keepdims=True)
        bias_sum += jnp.sum(dbranch.astype(wide), axis=0, keepdims=True)
    sums_ref[...] = jnp.zeros(sums_ref.shape, wide)
    sums_ref[0:1, :] = bias_sum
    sums_ref[1:2, :] = gain_sum
    sums_ref[2:3, :] = shift_sum


def final_norm(normed, near, core, across, small, cot, live, waits):
    rows, model = normed.shape
    return kernel_call(
        final_kernel,
        "final_norm",
        [normed, near, core, across, small, cot, live],
        [
            ((rows, model), low, hbm),
            ((rows, model), wide, hbm),
            ((rows, model), low),
            ((8, model), wide, hbm),
        ],
        far_in=[0, 4, 5, 6],
        waits=waits,
    )


def first_back_kernel(groups, *refs):
    dsum_ref, near_ref, core_ref, far_ref, unit_ref, inv_ref, small_ref, own_map, maps_ref = refs[:9]
    dfirst_ref, dmerged_ref, sums_ref = refs[9:12]
    dctx_refs = refs[12:]
    gain = small_ref[1:2, :]
    gain_sum = shift_sum = bias_sum = 0.0
    for rows in steps(dsum_ref.shape[0]):
        grad = near_ref[rows, :].astype(wide) + core_ref[rows, :].astype(wide)
        grad = dsum_ref[rows, :] + grad + far_ref[rows, :].astype(wide)
        unit = unit_ref[rows, :]
        dfirst = norm_back(grad, unit, inv_ref[rows, 0:1], gain)
        dfirst_ref[rows, :] = dfirst
        dmerged = dfirst.astype(low)
        dmerged_ref[rows, :] = dmerged
        gain_sum += jnp.sum(grad * unit, axis=0, keepdims=True)
        shift_sum += jnp.sum(grad, axis=0, keepdims=True)
        bias_sum += jnp.sum(dmerged.astype(wide), axis=0, keepdims=True)
    for j in range(groups):
        merge_map = maps_ref[j - 1] if j else own_map[...]
        dctx_refs[j][...] = dot_nt(dmerged_ref[...], merge_map).astype(low)
    sums_ref[...] = jnp.zeros(sums_ref.shape, wide)
    sums_ref[3:4, :] = bias_sum
    sums_ref[4:5, :] = gain_sum
    sums_ref[5:6, :] = shift_sum


def first_back(dsum, near, core, across, unit, inverse, small, own_map, maps, waits):
    rows, model = dsum.shape
    groups, width = maps.shape[0] + 1, own_map.shape[0]
    found = kernel_call(
        functools.partial(first_back_kernel, groups),
        "first_back",
        [dsum, near, core, across, unit, inverse, small, own_map, maps],
        [((rows, model), wide, hbm), ((rows, model), low), ((8, model), wide, hbm)]
        + [((rows, width), low)] * groups,
        waits=waits,
        far_in=[0, 4, 5, 6, 7, 8],
    )
    return found[0], found[1], found[2], found[3:]


def forward_kernel(a_ref, b_ref, inner_ref, outer_ref, bias_ref, act_ref, slope_ref, own_ref, other_ref):
    rows = a_ref.shape[0]
    for ref, out, at in ((a_ref, own_ref, 0), (b_ref, other_ref, rows)):
        pre = dot_nt(ref[...], inner_ref[...]) + bias_ref[...]
        upper = 0.5 + 0.5 * lax.erf(pre * 0.7071067811865476)
        active = (pre * upper).astype(low)
        slope = upper + pre * (0.3989422804014327 * jnp.exp(-0.5 * pre * pre))
        act_ref[at : at + rows, :] = active
        slope_ref[at : at + rows, :] = slope.astype(low)
        out[...] = dot(active, outer_ref[...]).astype(low)


def feed_forward(a, b, inner, outer, bias, waits=()):
    rows, model = a.shape
    hidden = inner.shape[0]
    return kernel_call(
        forward_kernel,
        "feed_forward",
        [a, b, inner, outer, bias],
        [((2 * rows, hidden), low, hbm)] * 2 + [((rows, model), low)] * 2,
        waits=waits,
        far_in=[0, 1],
    )


def backward_kernel(a_ref, b_ref, inner_ref, outer_ref, slope_ref, dinner_ref, own_ref, other_ref):
    rows = a_ref.shape[0]
    for ref, out, at in ((a_ref, own_ref, 0), (b_ref, other_ref, rows)):
        dactive = dot_nt(ref[...], outer_ref[...])
        dinner = (dactive * slope_ref[at : at + rows, :].astype(wide)).astype(low)
        dinner_ref[at : at + rows, :] = dinner
        out[...] = dot(dinner, inner_ref[...]).astype(low)


def feed_backward(a, b, inner, outer, slope, waits=()):
    rows, model = a.shape
    hidden = inner.shape[0]
    return kernel_call(
        backward_kernel,
        "feed_backward",
        [a, b, inner, outer, slope],
        [((2 * rows, hidden), low, hbm)] + [((rows, model), low)] * 2,
        waits=waits,
        far_in=[4],
    )


def grad_kernel(numbers, block, bias, split, *refs):
    hid, row_refs, refs = refs[:2], refs[2:6], refs[6:]
    got_ref, out_refs = (refs[0], refs[1:]) if split else (None, refs)
    model = out_refs[0].shape[-1]
    half = len(numbers) // len(out_refs)
    for k, number in enumerate(numbers):
        cols = slice(number * block, (number + 1) * block)
        total = sums = 0.0
        for i, ref in enumerate(hid):
            rows = ref.shape[0] // 2
            total += dot_tn(ref[:rows, cols], row_refs[2 * i][...])
            total += dot_tn(ref[rows:, cols], row_refs[2 * i + 1][...])
            if bias:
                sums += jnp.sum(ref[:, cols].astype(wide), axis=0, keepdims=True)
        out_ref, at = out_refs[k // half], k % half
        if split:
            total += got_ref[k, :block, :].astype(wide)
        out_ref[at, :block, :] = total.astype(low)
        if bias:
            sums = jnp.pad(sums, ((0, 15), (0, model - block)))
            if split:
                sums += got_ref[k, block:, :].astype(wide)
            out_ref[at, block:, :] = sums.astype(low)


def weight_grad(hid, row_list, block, numbers, bias, waits, got=None):
    model = row_list[0].shape[1]
    split = got is not None
    count = len(numbers) // (1 + split)
    found = kernel_call(
        functools.partial(grad_kernel, numbers, block, bias, split),
        "weight_grad",
        [*hid, *row_list] + [got] * split,
        [((count, block + 16 * bias, model), low)] * (1 + split),
        waits=waits,
    )
    return found if split else found[0]


def units_kernel(units, shares, slot, inner_ref, outer_ref, bias_ref, own_inner, own_outer, own_bias):
    for m in range(shares):
        at = pl.multiple_of((slot[0] ^ (m << 1)) * units, units)
        own_inner[m] = inner_ref[:, pl.ds(at, units)].T
        own_outer[m] = outer_ref[pl.ds(at, units), :]
        own_bias[m] = jnp.broadcast_to(bias_ref[:, pl.ds(at, units)], (16, units))


def own_units(slot, shares, innermap, outermap, innerbias, waits):
    model = innermap.shape[0]
    units = innermap.shape[1] // (2 * shares)
    if units % 128:
        found = []
        for m in range(shares):
            at = (slot[0] ^ (m << 1)) * units
            inner = lax.dynamic_slice_in_dim(innermap, at, units, 1).T
            outer = lax.dynamic_slice_in_dim(outermap, at, units, 0)
            bias = lax.dynamic_slice_in_dim(innerbias, at, units, 1)
            found.append((inner, outer, jnp.broadcast_to(bias, (16, units))))
        return [jnp.stack(pieces) for pieces in zip(*found)]
    return kernel_call(
        functools.partial(units_kernel, units, shares),
        "own_units",
        [innermap, outermap, innerbias],
        [((shares, units, model), low, hbm)] * 2 + [((shares, 16, units), innerbias.dtype, hbm)],
        scalars=[slot],
        waits=waits,
        far_in=[0, 1],
    )


def pack_inner_kernel(own_inner, own_bias, pack_ref):
    units = own_inner.shape[1]
    pack_ref[0, :units, :] = own_inner[0]
    pack_ref[0, units:, :] = jnp.zeros((16, pack_ref.shape[2]), low)
    pack_ref[0, units:, :units] = own_bias[0]


def pack_outer_kernel(own_outer, pack_ref):
    pack_ref[0] = own_outer[0]


def pack_inner(own):
    _, units, model = own[0].shape
    out = [((1, units + 16, model), low)]
    return kernel_call(pack_inner_kernel, "pack_inner", [own[0], own[2]], out)[0]


def pack_outer(own, waits):
    _, units, model = own[1].shape
    out = [((1, units, model), low)]
    return kernel_call(pack_outer_kernel, "pack_outer", [own[1]], out, waits=waits)[0]


def stack_kernel(*refs):
    count = len(refs) // 3
    for k in range(count):
        a_ref, b_ref, out_ref = refs[2 * k], refs[2 * k + 1], refs[2 * count + k]
        out_ref[: a_ref.shape[0]] = a_ref[...]
        out_ref[a_ref.shape[0] :] = b_ref[...]


def stack_pairs(pairs):
    return kernel_call(
        stack_kernel,
        "stack_pairs",
        [value for pair in pairs for value in pair],
        [((2 * a.shape[0], *a.shape[1:]), a.dtype) for a, _ in pairs],
    )


def join_kernel(units, masks, own_inner, own_outer, own_bias, *refs):
    parts, (inner_ref, outer_ref, bias_ref) = refs[:-3], refs[-3:]
    for m in range(own_inner.shape[0]):
        at, far = 2 * m * units, (2 * m + 1) * units
        inner_ref[at:far, :] = own_inner[m]
        outer_ref[at:far, :] = own_outer[m]
        bias_ref[:, at:far] = own_bias[m, 0:1, :].astype(wide)
    for which, (ref, order) in enumerate(zip(parts, masks)):
        for k, m in enumerate(order):
            far = (2 * m + 1) * units
            if which < 2:
                inner_ref[far : far + units, :] = ref[k, :units, :]
                bias_ref[:, far : far + units] = ref[k, units : units + 16, :units].astype(wide)[:1]
            else:
                outer_ref[far : far + units, :] = ref[k]


def join_units(own, parts, masks, waits):
    shares, units, model = own[0].shape
    hidden = 2 * shares * units
    return kernel_call(
        functools.partial(join_kernel, units, masks),
        "join_units",
        [*own, *parts],
        [((hidden, model), low)] * 2 + [((1, hidden), wide)],
        waits=waits,
        far_in=hbm,
    )


def slot_order(number, bits):
    return ((number & 1) << (bits - 1)) | (number >> 1)


def qkv_kernel(counts, slots, slot, *refs):
    out_ref, q_all, kv_all = refs[-3:]
    dq_ref, refs = refs[0], refs[1:-3]
    width, model = dq_ref.shape[-1], out_ref.shape[-1]
    q_all[...] = dq_ref[...].reshape(q_all.shape)
    q_sum = jnp.sum(q_all[...].astype(wide), axis=0, keepdims=True)
    q_grad = kv_grad = kv_sum = 0.0
    for i, count in enumerate(counts):
        dkv_ref, tok_refs, refs = refs[0], refs[1 : 1 + count], refs[1 + count :]
        kv_all[...] = dkv_ref[...].reshape(kv_all.shape)
        kv_sum += jnp.sum(kv_all[...].astype(wide), axis=0, keepdims=True)
        at = 0
        for tok_ref in tok_refs:
            there = slice(at, at + tok_ref.shape[0])
            at += tok_ref.shape[0]
            kv_grad += dot_tn(kv_all[there, :], tok_ref[...])
            if i == 0:
                q_grad += dot_tn(q_all[there, :], tok_ref[...])
    grad = jnp.concatenate([q_grad, kv_grad]).astype(low)
    sums = jnp.concatenate([q_sum, kv_sum], axis=1)
    bits = slots.bit_length() - 1
    block = 3 * width // slots
    for b in range(slots):
        at = slot_order(slot[0] ^ b, bits)
        out_ref[at, :block, :] = grad[b * block : (b + 1) * block]
        line = jnp.pad(sums[:, b * block : (b + 1) * block], ((0, 15), (0, model - block)))
        out_ref[at, pad16(block) :, :] = line.astype(low)


def qkv_grads(slot, slots, dq, pairs, waits):
    model = pairs[0][1][0].shape[-1]
    groups, width = dq.shape[0], dq.shape[-1]
    total = dq.size // width
    far_at, at = [], 1
    for dkv, tok in pairs:
        far_at += range(at + 1, at + 1 + len(tok))
        at += 1 + len(tok)
    return kernel_call(
        functools.partial(qkv_kernel, [len(tok) for _, tok in pairs], slots),
        "qkv_grads",
        [dq] + [a for dkv, tok in pairs for a in (dkv, *tok)],
        [((slots, pad16(3 * width // slots) + 16, model), low)],
        far_in=far_at,
        scalars=[slot],
        waits=waits,
        scratch=[pltpu.VMEM((total, width), low), pltpu.VMEM((total, 2 * width), low)],
        mebibytes=24,
    )[0]


def hold_kernel(value_ref, out_ref):
    out_ref[...] = value_ref[...]


def hold(value, waits):
    out = [(value.shape, value.dtype)]
    return kernel_call(hold_kernel, "hold", [value], out, waits=waits)[0]


def add_kernel(a_ref, b_ref, *out_refs):
    at = 0
    for ref in out_refs:
        there = slice(at, at + ref.shape[0])
        at += ref.shape[0]
        ref[...] = (a_ref[there].astype(wide) + b_ref[there].astype(wide)).astype(ref.dtype)


def add_split(a, b, counts, waits=(), kind=low):
    out = [((count, *a.shape[1:]), kind) for count in counts]
    return kernel_call(add_kernel, "add_split", [a, b], out, waits=waits)


def dtokens_kernel(dq_ref, own_ref, got_ref, q_ref, k_ref, v_ref, *out_refs):
    width = dq_ref.shape[-1]
    rows = dq_ref.shape[1] * dq_ref.shape[2]
    for j, ref in enumerate(out_refs):
        dkv = (own_ref[j].astype(wide) + got_ref[j].astype(wide)).astype(low)
        dkv = dkv.reshape(rows, 2 * width)
        total = dot_nt(dq_ref[j].reshape(rows, width), q_ref[...])
        total += dot_nt(dkv[:, :width], k_ref[...]) + dot_nt(dkv[:, width:], v_ref[...])
        ref[...] = total.astype(ref.dtype)


def dtokens(dq, own, got, maps, waits):
    rows, model = dq.shape[1] * dq.shape[2], maps[0].shape[0]
    return kernel_call(
        dtokens_kernel,
        "dtokens",
        [dq, own, got, *maps],
        [((rows, model), wide), ((rows, model), low)] * (dq.shape[0] // 2),
        waits=waits,
    )


def tokens_kernel(dfirst_ref, part_ref, near_ref, far_ref, out_ref):
    total = dfirst_ref[...] + part_ref[...] + near_ref[...].astype(wide)
    out_ref[...] = (total + far_ref[...].astype(wide)).astype(low)


def pack_sums_kernel(units, inner_ref, inner_got, outer_ref, outer_got, own_ref, send_ref):
    model = own_ref.shape[1]
    inner = inner_ref[0].astype(wide) + inner_got[0].astype(wide)
    outer = outer_ref[0].astype(wide) + outer_got[0].astype(wide)
    sums = inner[2 * units :, : 2 * units].astype(low)
    for k, ref in enumerate((own_ref, send_ref)):
        there = slice(k * units, (k + 1) * units)
        ref[:units, :] = inner[there].astype(low)
        ref[units : 2 * units, :] = outer[there].astype(low)
        ref[2 * units :, :] = jnp.zeros((16, model), low)
        ref[2 * units :, :units] = sums[:, there]


def pack_sums(units, inner, inner_got, outer, outer_got, waits):
    model = inner.shape[-1]
    return kernel_call(
        functools.partial(pack_sums_kernel, units),
        "pack_sums",
        [inner, inner_got, outer, outer_got],
        [((2 * units + 16, model), low)] * 2,
        waits=waits,
    )


def merge_grad_kernel(groups, core, *refs):
    ctx_refs, (dmerged_ref, a_ref, b_ref, keep_ref, send_ref, grad_all) = refs[:groups], refs[groups:]
    half = keep_ref.shape[1]
    for j, ref in enumerate(ctx_refs):
        grad_all[...] = dot_tn(ref[...], dmerged_ref[...]).astype(low)
        keep = pl.multiple_of(core[0] * half, half)
        send = pl.multiple_of((1 - core[0]) * half, half)
        keep_ref[j] = grad_all[pl.ds(keep, half), :]
        send_ref[j * half : (j + 1) * half, :] = grad_all[pl.ds(send, half), :]
    sums = a_ref[...] + b_ref[...]
    send_ref[groups * half :, :] = jnp.concatenate([sums, jnp.zeros_like(sums)]).astype(low)


def merge_grads(core, ctx, dmerged, a, b):
    rows, width = ctx[0].shape
    model = dmerged.shape[1]
    groups, half = len(ctx), width // 2
    return kernel_call(
        functools.partial(merge_grad_kernel, groups),
        "merge_grads",
        [*ctx, dmerged, a, b],
        [((groups, half, model), low), ((groups * half + 16, model), low)],
        far_in=[i for i in range(groups + 3) if i != groups],
        scalars=[core],
        scratch=[pltpu.VMEM((width, model), low)],
    )


def merge_heads_kernel(groups, a_ref, b_ref, keep_ref, got_ref, near_ref, send_ref, sums_ref):
    half = keep_ref.shape[1]
    total = lambda j: keep_ref[j].astype(wide) + got_ref[j * half : (j + 1) * half, :].astype(wide)
    for k in range(groups // 2):
        near_ref[k] = total(2 * k).astype(low)
        send_ref[k * half : (k + 1) * half, :] = total(2 * k + 1).astype(low)
    sums = a_ref[...] + b_ref[...] + got_ref[groups * half : groups * half + 16, :].astype(wide)[:8]
    sums_ref[...] = sums
    at = groups // 2 * half
    send_ref[at:, :] = jnp.concatenate([sums, jnp.zeros_like(sums)]).astype(low)


def merge_heads(a, b, keep, got):
    groups, half, model = keep.shape
    count = groups // 2
    return kernel_call(
        functools.partial(merge_heads_kernel, groups),
        "merge_heads",
        [a, b, keep, got],
        [((count, half, model), low), ((count * half + 16, model), low), ((8, model), wide)],
    )


def merge_far_kernel(keep_ref, got_ref, sums_ref, near_ref, send_ref, out_sums_ref):
    half = keep_ref.shape[1]
    near_ref[...] = (keep_ref[0].astype(wide) + got_ref[:half, :].astype(wide)).astype(low)
    far = keep_ref[1].astype(wide) + got_ref[half : 2 * half, :].astype(wide)
    send_ref[:half, :] = far.astype(low)
    sums = sums_ref[...] + got_ref[2 * half :, :].astype(wide)[:8]
    out_sums_ref[...] = sums
    send_ref[half:, :] = jnp.concatenate([sums, jnp.zeros_like(sums)]).astype(low)


def merge_far(keep, got, sums, waits):
    _, half, model = keep.shape
    return kernel_call(
        merge_far_kernel,
        "merge_far",
        [keep, got, sums],
        [((half, model), low), ((half + 16, model), low), ((8, model), wide)],
        waits=waits,
    )


def slots_kernel(block, size, slot, grad_ref, core_ref, near_ref, far_ref, sums_ref, *refs):
    own_ref, send_refs, (out_sums_ref, rows_all) = refs[0], refs[1:-2], refs[-2:]
    shares = len(send_refs) + 1
    half = near_ref.shape[0]
    merged = (near_ref[...].astype(wide) + far_ref[:half, :].astype(wide)).astype(low)
    for k in range(shares):
        rows_all[k] = merged[k * size : (k + 1) * size]
    sums = sums_ref[...] + far_ref[half:, :].astype(wide)[:8]
    out_sums_ref[...] = sums
    start = pad16(block) + 16
    for m, ref in enumerate((own_ref, *send_refs)):
        ref[:start, :] = (grad_ref[m].astype(wide) + core_ref[m].astype(wide)).astype(low)
        ref[start : start + size, :] = rows_all[(slot[0] >> 1) ^ m]
        if m:
            both = jnp.concatenate([sums, jnp.zeros_like(sums)]).astype(low)
            ref[start + pad16(size) :, :] = both


def slot_parts(slot, block, size, grads, core, near, far, sums, waits):
    shares, _, model = core.shape
    rows = pad16(block) + 16 + pad16(size)
    return kernel_call(
        functools.partial(slots_kernel, block, size),
        "slot_parts",
        [grads, core, near, far, sums],
        [((rows, model), low)]
        + [((rows + 16, model), low)] * (shares - 1)
        + [((8, model), wide)],
        scalars=[slot],
        scratch=[pltpu.VMEM((shares, size, model), low)],
        waits=waits,
    )


def slot_sum_kernel(own_ref, sums_ref, *refs):
    got_refs, (out_ref, out_sums_ref) = refs[:-2], refs[-2:]
    rows = own_ref.shape[0]
    total, sums = own_ref[...].astype(wide), sums_ref[...]
    for ref in got_refs:
        total += ref[:rows, :].astype(wide)
        sums += ref[rows:, :].astype(wide)[:8]
    out_ref[...] = total.astype(low)
    out_sums_ref[...] = sums


def slot_sum(own, sums, got, waits):
    return kernel_call(
        slot_sum_kernel,
        "slot_sum",
        [own, sums, *got],
        [(own.shape, low), (sums.shape, wide)],
        waits=waits,
    )


def feed_out_kernel(units, grads_ref, inner_ref, outer_ref, bias_ref, here, inner, outer, bias, sems):
    slots, rows, model = grads_ref.shape
    copies = [pltpu.make_async_copy(grads_ref.at[k], here.at[k], sems.at[0, k]) for k in range(slots)]
    for copy in copies:
        copy.start()
    done = []
    for k, copy in enumerate(copies):
        copy.wait()
        cols = slice(k * units, (k + 1) * units)
        inner[:, cols] = here[k, :units, :].astype(wide).T
        outer[cols, :] = here[k, units : 2 * units, :].astype(wide)
        bias[k : k + 1, :] = here[k, 2 * units : 2 * units + 16, :units].astype(wide)[:1]
        done.append(pltpu.make_async_copy(inner.at[:, cols], inner_ref.at[:, cols], sems.at[1, k]))
        done.append(pltpu.make_async_copy(outer.at[cols, :], outer_ref.at[cols, :], sems.at[2, k]))
        done[-2].start()
        done[-1].start()
    done.append(pltpu.make_async_copy(bias, bias_ref, sems.at[0, 0]))
    done[-1].start()
    for copy in done:
        copy.wait()


def feed_out(grads, units):
    slots, rows, model = grads.shape
    hidden = slots * units
    if units % 128:
        inner = grads[:, :units].reshape(hidden, model).astype(wide).T
        outer = grads[:, units : 2 * units].reshape(hidden, model).astype(wide)
        return inner, outer, grads[:, 2 * units, :units].astype(wide)
    shapes = [(model, hidden), (hidden, model), (slots, units)]
    return pl.pallas_call(
        functools.partial(feed_out_kernel, units),
        in_specs=[in_hbm],
        out_specs=[in_hbm] * 3,
        out_shape=[jax.ShapeDtypeStruct(shape, wide) for shape in shapes],
        scratch_shapes=[pltpu.VMEM(grads.shape, low)]
        + [pltpu.VMEM(shape, wide) for shape in shapes]
        + [pltpu.SemaphoreType.DMA((3, slots))],
        compiler_params=params(60),
        name="feed_out",
    )(grads)


def qkv_out_kernel(block, order, slot, *refs):
    parts, refs = refs[: len(order)], refs[len(order) :]
    q_ref, k_ref, v_ref, merge_ref, bias_ref, rows_all, merge_all = refs
    start, size = pad16(block), merge_all.shape[1]
    width = q_ref.shape[1]
    slots = merge_all.shape[0]
    for mask, part in zip(order, parts):
        at = slot[0] ^ mask
        rows_all[at] = part[:block, :]
        bias_ref[pl.ds(at, 1), :] = part[start : start + 16, :].astype(wide)[:1]
        at = (at & 1) * (slots // 2) + (at >> 1)
        merge_all[at] = part[start + 16 : start + 16 + size, :]
    grad = rows_all[...].reshape(3 * width, -1)
    for i, ref in enumerate((q_ref, k_ref, v_ref)):
        ref[...] = grad[i * width : (i + 1) * width].astype(wide).T
    merge_ref[...] = merge_all[...].reshape(merge_ref.shape).astype(wide)


def qkv_out(slot, parts, order, block, width):
    model = parts[0].shape[-1]
    slots = 3 * width // block
    size = width // slots
    return kernel_call(
        functools.partial(qkv_out_kernel, block, order),
        "qkv_out",
        parts,
        [((model, width), wide)] * 3 + [((width, model), wide), ((slots, model), wide)],
        scalars=[slot],
        scratch=[pltpu.VMEM((slots, block, model), low), pltpu.VMEM((slots, size, model), low)],
    )


def shards(
    tokens,
    querymap,
    querybias,
    keymap,
    valuemap,
    valuebias,
    mergemap,
    mergebias,
    normgain,
    normshift,
    innermap,
    innerbias,
    outermap,
    outerbias,
    finalgain,
    finalshift,
    lengths,
    cotangent,
):
    proteins, share, model = tokens.shape
    groups = lax.axis_size("heads")
    rows = proteins * share
    width = querymap.shape[1]
    seq, heads = lax.axis_index("seq"), lax.axis_index("heads")
    seq_size, dp_size = lax.axis_size("seq"), lax.axis_size("dp")
    pos = jnp.concatenate([lengths, jnp.stack([seq, heads]).astype(jnp.int32)])
    core_bit, row_bit, far_bit = ("seq", 1), ("heads", 1), ("heads", 2)
    seq_bits = [("seq", 1 << k) for k in range(1, seq_size.bit_length() - 1)]
    share_bits = seq_bits + [("dp", 1 << k) for k in range(dp_size.bit_length() - 1)]
    slot_bits = [core_bit] + share_bits
    slots = 1 << len(slot_bits)
    shares = slots // 2
    slot = lax.axis_index("dp") * seq_size + seq
    units = innermap.shape[1] // slots
    merge_units = width // slots
    row = lambda vector: vector.reshape(1, -1)

    slot_scalar = slot.reshape(1).astype(jnp.int32)

    own_rows = tokens.reshape(rows, model)
    small = jnp.stack([mergebias, normgain, normshift, outerbias, finalgain, finalshift])
    small = jnp.pad(small.astype(wide), ((0, 2), (0, 0)))
    second = swap(own_rows, *far_bit)
    first = swap(own_rows, *row_bit)
    maps = [querymap, keymap, valuemap]
    biases = [row(querybias), row(valuebias)]
    merge_own = lax.dynamic_slice_in_dim(mergemap, slot * merge_units, merge_units, 0)
    merge_all = lax.all_gather(merge_own, ("dp", "seq", "heads"))
    merge_all = merge_all.reshape(slots, groups, merge_units, model)
    own = own_units(slot_scalar, shares, innermap, outermap, row(innerbias), [small])

    def exchange_keys(piece):
        found = {0: piece}
        for axis, stride in seq_bits + [core_bit]:
            for i in list(found):
                found[i | stride] = swap(found[i], axis, stride)
        return found

    maps_biases = [*maps, *biases]
    seq_tokens = {i: [] for i in range(0, seq_size, 2)}

    def exchange_tokens(piece):
        found = {0: piece}
        for axis, stride in seq_bits:
            for i in list(found):
                found[i | stride] = swap(found[i], axis, stride)
        for i in found:
            seq_tokens[i].append(found[i])
        return [found[i] for i in found if i]

    far_tokens = [exchange_tokens(own_rows)]
    far_inner = swap(pack_inner(own), *far_bit)
    second_held = hold(second, [first, own[0]])
    third = swap(second_held, *row_bit)
    q_three, kv_three = project([own_rows, first, second_held], maps_biases, proteins)
    kv_three = exchange_keys(kv_three)
    q_last, kv_last = project([third], maps_biases, proteins, [q_three])
    kv_last = exchange_keys(kv_last)
    queries = [q_three, q_last]
    kv_pieces = [stack[i] for i in range(seq_size) for stack in (kv_three, kv_last)]
    token_pieces = [own_rows, first, second, third]
    far_outer = swap(pack_outer(own, [third]), *far_bit)
    pairs = [far_inner, far_outer]
    order = list(range(len(share_bits)))
    masks = [[0], [0]]
    for k, bits in enumerate(zip(order, order[::-1])):
        if k:
            pairs = stack_pairs(pairs)
        pairs = [(p, swap(p, *share_bits[bit])) for p, bit in zip(pairs, bits)]
        masks = [(have, [m | (1 << bit) for m in have]) for have, bit in zip(masks, bits)]
        if k < len(order) - 1:
            masks = [a + b for a, b in masks]
    far_tokens += [exchange_tokens(piece) for piece in token_pieces[1:]]

    stacked = [p for pair in pairs for p in pair[:1]]
    context, context_t, logsum = attend(pos, queries, kv_pieces, stacked)
    context = [c.reshape(rows, width) for c in context]
    context = [context[0]] + [swap(context[j], "heads", j) for j in range(1, groups)]
    normed, normed_low, first_unit, first_inverse, other_maps = merge_norm(
        heads.reshape(1).astype(jnp.int32),
        context,
        mergemap,
        merge_all,
        own_rows,
        small,
        [],
    )
    inner_t, outer_w, inner_b = join_units(
        own, [p for pair in pairs for p in pair], [m for pair in masks for m in pair], [normed_low]
    )

    normed_near, normed_across = swap(normed_low, *core_bit), swap(normed_low, *row_bit)
    near_act, near_slope, near_own, near_other = feed_forward(
        normed_low, normed_near, inner_t, outer_w, inner_b
    )
    normed_across = hold(normed_across, [near_act, *far_tokens[1]])
    normed_both = swap(normed_across, *core_bit)
    normed_rows = [normed_low, normed_near, normed_across, normed_both]
    far_act, far_slope, far_own, far_other = feed_forward(
        normed_across, normed_both, inner_t, outer_w, inner_b, [near_act]
    )
    (far_part,) = add_split(far_own, swap(far_other, *core_bit), [rows])
    far_sum = swap(far_part, *row_bit)
    own_at = (seq * groups + heads) * share + jnp.arange(share, dtype=jnp.int32)
    live = (own_at[None, :] < lengths[:, None]).astype(wide).reshape(rows, 1)
    layer_output, dsum_final, dbranch, final_sums = final_norm(
        normed,
        near_own,
        swap(near_other, *core_bit),
        far_sum,
        small,
        cotangent.reshape(rows, model),
        jnp.broadcast_to(live, (rows, 128)),
        far_tokens[2],
    )
    dbranch_near, dbranch_across = swap(dbranch, *core_bit), swap(dbranch, *row_bit)
    near_dinner, near_own, near_other = feed_backward(
        dbranch, dbranch_near, inner_t, outer_w, near_slope
    )
    dbranch_across = hold(dbranch_across, [near_dinner, *far_tokens[3]])
    dbranch_both = swap(dbranch_across, *core_bit)
    dbranch_rows = [dbranch, dbranch_near, dbranch_across, dbranch_both]
    hid_block = 2 * units
    last = len(share_bits) - 1
    numbers = lambda k, side: [m for m in range(shares) if (m >> k) & 1 == side]
    acts = [near_act, far_act]
    far_dinner, far_own, far_other = feed_backward(
        dbranch_across,
        dbranch_both,
        inner_t,
        outer_w,
        far_slope,
        [near_dinner],
    )
    (far_part,) = add_split(far_own, swap(far_other, *core_bit), [rows])
    far_sum = swap(far_part, *row_bit)

    dinners = [near_dinner, far_dinner]
    outer_send = weight_grad(acts, dbranch_rows, hid_block, numbers(last, 1), 0, [far_part])
    outer_got = swap(outer_send, *share_bits[last])
    inner_send = weight_grad(dinners, normed_rows, hid_block, numbers(0, 1), 1, [far_part])
    inner_got = swap(inner_send, *share_bits[0])
    dfirst, dmerged, first_sums, dcontext = first_back(
        dsum_final,
        near_own,
        swap(near_other, *core_bit),
        far_sum,
        first_unit,
        first_inverse,
        small,
        mergemap,
        other_maps,
        [inner_send, *far_tokens[0]],
    )
    dcontext = [dcontext[0]] + [swap(dcontext[j], "heads", j) for j in range(1, groups)]
    dcontext = [d.reshape(proteins, share, width) for d in dcontext]
    core = bit_of(core_bit).reshape(1).astype(jnp.int32)
    merge_keep, merge_send = merge_grads(core, context, dmerged, final_sums, first_sums)
    merge_keep, merge_send, sums = merge_heads(
        final_sums, first_sums, merge_keep, swap(merge_send, *core_bit)
    )
    merge_got = swap(merge_send, *row_bit)
    outer_keep = weight_grad(acts, dbranch_rows, hid_block, numbers(last, 0), 0, [dmerged])
    inner_keep = weight_grad(dinners, normed_rows, hid_block, numbers(0, 0), 1, [outer_keep])
    merge_near, merge_send, sums = merge_far(
        merge_keep, merge_got, sums, [outer_keep, inner_keep]
    )
    merge_got = swap(merge_send, *far_bit)

    def shared_sum(hid, row_list, got, k, bias, waits):
        bits = [b for i, b in enumerate(share_bits) if i != k]
        if not bits:
            (keep,) = weight_grad(hid, row_list, hid_block, numbers(k, 0), bias, waits)
            return keep, got
        half = hid.shape[0] // 2
        keep, send = add_split(hid, got, [half, half], waits)
        got = swap(send, *bits[-1])
        for bit in reversed(bits[:-1]):
            half = keep.shape[0] // 2
            keep, send = add_split(keep, got, [half, half])
            got = swap(send, *bit)
        return keep, got

    outer_sums = shared_sum(outer_keep, dbranch_rows, outer_got, last, 0, [merge_send])
    inner_sums = shared_sum(inner_keep, normed_rows, inner_got, 0, 1, [merge_send])

    dqueries, dkv_by_seq = attend_back(
        pos, queries, dcontext, context_t, logsum, kv_pieces, [outer_sums[0], inner_sums[0], merge_send]
    )
    half = groups // 2
    dkv_by_seq = list(dkv_by_seq)
    dkv_by_seq[1::2] = gate(dkv_by_seq[1::2], [inner_sums[1], outer_sums[1], merge_got])
    own_pack, send_pack = pack_sums(units, *inner_sums, *outer_sums, [dqueries])
    far_pack = swap(send_pack, *far_bit)
    dkv_parts = [
        add_split(dkv_by_seq[i], swap(dkv_by_seq[i + 1], *core_bit), [groups])[0]
        for i in range(0, seq_size, 2)
    ]
    pairs = list(zip(dkv_parts, [seq_tokens[i] for i in range(0, seq_size, 2)]))
    slot_grads = qkv_grads(slot_scalar, slots, dqueries, pairs, [send_pack])
    block = 3 * width // slots
    slot_send = slot_parts(
        slot_scalar,
        block,
        merge_units,
        slot_grads,
        swap(slot_grads[shares:], *core_bit),
        merge_near,
        merge_got,
        sums,
        [],
    )
    slot_got = [swap_slots(slot_send[m], m << 1) for m in range(1, shares)]
    parts = dkv_parts
    for k in reversed(range(len(seq_bits))):
        count = 1 << k
        got = [swap(parts[count + i], *seq_bits[k]) for i in range(count)]
        if k:
            parts = [add_split(parts[i], got[i], [groups])[0] for i in range(count)]

    got[:1] = gate(got[:1], slot_got)

    part_none, part_one, part_two, part_three = dtokens(
        dqueries, parts[0], got[0], maps, [slot_send[0]]
    )
    rest = swap(part_three, *row_bit)
    near = swap(part_one, *row_bit)
    out_pack, extra = slot_sum(slot_send[0], slot_send[-1], slot_got, [part_three])
    (far_send,) = add_split(part_two, rest, [rows], [out_pack])
    far = swap(far_send, *far_bit)

    (pack,) = add_split(own_pack, far_pack, [own_pack.shape[0]], [part_three])
    grads = lax.all_gather(pack, ("dp", "seq"))

    parts = [out_pack] + [swap_slots(out_pack, m << 1) for m in range(1, shares)]
    order = [m << 1 for m in range(shares)]
    q_grad, k_grad, v_grad, mergemap_grad, bias_rows = qkv_out(
        slot_scalar,
        parts + [swap(part, *core_bit) for part in parts],
        order + [m | 1 for m in order],
        block,
        width,
    )
    tokens_grad = kernel_call(
        tokens_kernel, "tokens_grad", [dfirst, part_none, near, far], [((rows, model), low)]
    )[0]
    innermap_grad, outermap_grad, innerbias_grad = feed_out(grads, units)
    innerbias_grad = innerbias_grad.reshape(-1)
    bias_grads = bias_rows[:, :block].reshape(-1)
    shape = tokens.shape
    return (
        layer_output.reshape(shape),
        tokens_grad.reshape(shape),
        q_grad,
        bias_grads[:width],
        k_grad,
        v_grad,
        bias_grads[2 * width :],
        mergemap_grad,
        extra[3],
        extra[4],
        extra[5],
        innermap_grad,
        innerbias_grad,
        outermap_grad,
        extra[0],
        extra[1],
        extra[2],
    )


def solution(mesh):
    return jax.shard_map(
        shards,
        mesh=mesh,
        in_specs=(
            P("dp", ("seq", "heads"), None),
            P(None, "heads"),
            P("heads"),
            P(None, "heads"),
            P(None, "heads"),
            P("heads"),
            P("heads", None),
            P(),
            P(),
            P(),
            P(None, "heads"),
            P("heads"),
            P("heads", None),
            P(),
            P(),
            P(),
            P("dp"),
            P("dp", ("seq", "heads"), None),
        ),
        out_specs=(
            P("dp", ("seq", "heads"), None),
            P("dp", ("seq", "heads"), None),
            P(None, "heads"),
            P("heads"),
            P(None, "heads"),
            P(None, "heads"),
            P("heads"),
            P("heads", None),
            P(),
            P(),
            P(),
            P(None, "heads"),
            P("heads"),
            P("heads", None),
            P(),
            P(),
            P(),
        ),
        check_vma=False,
    )
```

profile of v0, /device:TPU:0, one launch (start us, length us, event | category | flops | bytes accessed | tf_op | source)
XLA Modules:
  0.0 369.9 jit_solution(9593551403194776883)
XLA Ops:
  7.2 1.5 constant_dynamic-slice_fusion
  8.8 3.1 collective-permute-start
  11.9 2.6 collective-permute-start.1
  19.4 1.6 copy-done.48
  21.0 1.6 copy-done.49
  24.5 11.8 %collective-permute-done.refs_1_.refs_4_ = bf16[256,1024]{1,0:T(8,128)(2,1)S(1)} collective-permute-done((bf16[256,1024]{1,0:T(8,128)(2,1)}, bf16[256,1024]{1,0:T(8,128)(2,1)S(1)}, u32[]{:S(2)}, u32[]{:S(2)}) %collective-permute-start) | collective-permute-done | bytes 524320 | tf_op jit(solution)/shard_map/ppermute | solution.py:35
  36.3 2.6 collective-permute-done.1.refs_0_.refs_5_
  39.8 4.2 %project.2 = (bf16[3,4,64,256]{3,2,1,0:T(8,128)(2,1)}, bf16[3,4,64,512]{3,2,1,0:T(8,128)(2,1)}) custom-call(bf16[256,1024]{1,0:T(8,128)(2,1)} %bitcast.2.refs_0_.refs_7_.refs_3_, bf16[256,1024]{1,0:T(8,128)(2,1)} %copy-done.19, bf16[256,1024]{1,0:T(8,128)(2,1)} %copy-done.50, bf16[1024,256]{1,0:T(8,128)(2,1)} %refs_3_.5, bf16[1024,256]{1,0:T(8,128)(2,1)} %refs_4_.3, ...), custom_call_target="tpu_custom_call" | custom-call | flops 1 | bytes 1 | tf_op jit(solution)/shard_map/project/pallas_call | solution.py:98
  44.0 1.6 collective-permute-start.9
  46.5 2.9 collective-permute-start.3
  49.4 12.9 %collective-permute-done.9.refs_9_.refs_16_ = bf16[3,4,64,512]{3,2,1,0:T(8,128)(2,1)} collective-permute-done((bf16[3,4,64,512]{3,2,1,0:T(8,128)(2,1)}, bf16[3,4,64,512]{3,2,1,0:T(8,128)(2,1)}, u32[]{:S(2)}, u32[]{:S(2)}) %collective-permute-start.9) | collective-permute-done | bytes 786464 | tf_op jit(solution)/shard_map/ppermute | solution.py:35
  62.3 2.9 collective-permute-done.3.refs_0_
  66.0 3.2 collective-permute-start.5
  69.3 2.9 project.3
  72.2 1.5 collective-permute-start.10
  73.6 9.2 %collective-permute-done.5.refs_2_ = bf16[1,128,1024]{2,1,0:T(8,128)(2,1)S(1)} collective-permute-done((bf16[1,128,1024]{2,1,0:T(8,128)(2,1)S(1)}, bf16[1,128,1024]{2,1,0:T(8,128)(2,1)S(1)}, u32[]{:S(2)}, u32[]{:S(2)}) %collective-permute-start.5) | collective-permute-done | bytes 262176 | tf_op jit(solution)/shard_map/ppermute | solution.py:35
  82.8 1.5 collective-permute-start.6
  85.4 4.5 %collective-permute-done.6.refs_3_ = bf16[1,128,1024]{2,1,0:T(8,128)(2,1)S(1)} collective-permute-done((bf16[1,128,1024]{2,1,0:T(8,128)(2,1)S(1)}, bf16[1,128,1024]{2,1,0:T(8,128)(2,1)S(1)}, u32[]{:S(2)}, u32[]{:S(2)}) %collective-permute-start.6) | collective-permute-done | bytes 262176 | tf_op jit(solution)/shard_map/ppermute | solution.py:35
  90.7 2.2 stack_pairs.1
  93.8 9.6 %attend.1 = (bf16[4,64,256]{2,1,0:T(8,128)(2,1)}, bf16[4,64,256]{2,1,0:T(8,128)(2,1)}, bf16[4,64,256]{2,1,0:T(8,128)(2,1)}, bf16[4,64,256]{2,1,0:T(8,128)(2,1)},...) custom-call(s32[6]{0:T(128)} %pad_add_fusion.refs_0_, bf16[3,4,64,256]{3,2,1,0:T(8,128)(2,1)} %get-tuple-element.106.refs_6_.refs_1_, ...), custom_call_target="tpu_custom_call" | custom-call | flops 10000000000 | bytes 1 | tf_op jit(solution)/shard_map/attend/pallas_call | solution.py:98
  103.5 1.6 collective-permute-start.14
  105.1 2.8 collective-permute-start.15
  108.6 2.6 collective-permute-start.18
  111.3 3.8 %collective-permute-done.14.refs_3_ = bf16[256,256]{1,0:T(8,128)(2,1)S(1)} collective-permute-done((bf16[256,256]{1,0:T(8,128)(2,1)}, bf16[256,256]{1,0:T(8,128)(2,1)S(1)}, u32[]{:S(2)}, u32[]{:S(2)}) %collective-permute-start.14) | collective-permute-done | bytes 131104 | tf_op jit(solution)/shard_map/ppermute | solution.py:35
  115.8 5.3 %merge_norm.1 = (f32[256,1024]{1,0:T(8,128)}, bf16[256,1024]{1,0:T(8,128)(2,1)}, f32[256,1024]{1,0:T(8,128)}, f32[256,128]{1,0:T(8,128)}, bf16[3,256,1024]{2,1,0:T(8,128)(2,1)}) custom-call(s32[1]{0:T(128)} %bitcast.refs_0_, bf16[256,256]{1,0:T(8,128)(2,1)} %bitcast.25, bf16[256,256]{1,0:T(8,128)(2,1)} %copy-done.76, bf16[256,256]{1,0:T(8,128)(2,1)} %copy-done.78, ...), custom_call_target="tpu_custom_call" | custom-call | flops 1 | bytes 1 | tf_op jit(solution)/shard_map/merge_norm/pallas_call | solution.py:98
  121.2 3.5 collective-permute-start.21
  124.8 2.1 collective-permute-start.20
  127.7 4.4 %join_units.1 = (bf16[1024,1024]{1,0:T(8,128)(2,1)}, bf16[1024,1024]{1,0:T(8,128)(2,1)}, f32[1,1024]{1,0:T(1,128)}) custom-call(bf16[4,128,1024]{2,1,0:T(8,128)(2,1)} %copy-done.7, bf16[4,128,1024]{2,1,0:T(8,128)(2,1)} %copy-done.37, bf16[4,16,128]{2,1,0:T(8,128)(2,1)} %copy-done.88, bf16[2,144,1024]{2,1,0:T(8,128)(2,1)} %get-tuple-element.110.refs_3_, ...), custom_call_target="tpu_custom_call" | custom-call | flops 1 | bytes 1 | tf_op jit(solution)/shard_map/join_units/pallas_call | solution.py:98
  132.1 1.6 copy-done
  133.7 1.6 copy-done.2
  136.0 3.6 feed_forward.2
  141.3 1.6 hold.4.refs_0_.refs_4_
  143.0 1.9 collective-permute-done.22.refs_1_.refs_5_
  144.9 2.9 feed_forward.3
  152.9 11.2 %collective-permute-done.25.refs_7_.refs_10_ = bf16[256,1024]{1,0:T(8,128)(2,1)S(1)} collective-permute-done((bf16[256,1024]{1,0:T(8,128)(2,1)S(1)}, bf16[256,1024]{1,0:T(8,128)(2,1)S(1)}, u32[]{:S(2)}, u32[]{:S(2)}) %collective-permute-start.25) | collective-permute-done | bytes 524320 | tf_op jit(solution)/shard_map/ppermute | solution.py:35
  164.1 2.9 collective-permute-done.24.refs_3_
  170.4 3.1 final_norm.1
  176.4 3.2 feed_backward.2
  180.4 8.6 %collective-permute-done.29.refs_2_.refs_11_ = bf16[256,1024]{1,0:T(8,128)(2,1)S(1)} collective-permute-done((bf16[256,1024]{1,0:T(8,128)(2,1)}, bf16[256,1024]{1,0:T(8,128)(2,1)S(1)}, u32[]{:S(2)}, u32[]{:S(2)}) %collective-permute-start.29) | collective-permute-done | bytes 524320 | tf_op jit(solution)/shard_map/ppermute | solution.py:35
  189.3 1.9 collective-permute-done.30.refs_1_.refs_5_
  191.2 2.6 feed_backward.3
  202.7 6.7 %collective-permute-done.33.refs_10_.refs_8_ = bf16[256,1024]{1,0:T(8,128)(2,1)} collective-permute-done((bf16[256,1024]{1,0:T(8,128)(2,1)}, bf16[256,1024]{1,0:T(8,128)(2,1)}, u32[]{:S(2)}, u32[]{:S(2)}) %collective-permute-start.33) | collective-permute-done | bytes 524320 | tf_op jit(solution)/shard_map/ppermute | solution.py:35
  209.5 1.5 collective-permute-done.32.refs_3_
  211.1 2.9 first_back.1
  219.4 1.7 collective-permute-start.34
  221.3 16.1 %collective-permute-done.39.refs_1_ = bf16[272,1024]{1,0:T(8,128)(2,1)S(1)} collective-permute-done((bf16[272,1024]{1,0:T(8,128)(2,1)S(1)}, bf16[272,1024]{1,0:T(8,128)(2,1)S(1)}, u32[]{:S(2)}, u32[]{:S(2)}) %collective-permute-start.39) | collective-permute-done | bytes 557088 | tf_op jit(solution)/shard_map/ppermute | solution.py:35
  246.7 12.6 %attend_back.1 = (bf16[4,4,64,256]{3,2,1,0:T(8,128)(2,1)}, bf16[4,4,64,512]{3,2,1,0:T(8,128)(2,1)}, bf16[4,4,64,512]{3,2,1,0:T(8,128)(2,1)}, bf16[4,4,64,512]{3,2,1,0:T(8,128)(2,1)}, bf16[4,4,64,512]{3,2,1,0:T(8,128)(2,1)}) custom-call(s32[6]{0:T(128)} %pad_add_fusion.refs_0_, bf16[3,4,64,256]{3,2,1,0:T(8,128)(2,1)} %get-tuple-element.106.refs_6_.refs_1_, ...), custom_call_target="tpu_custom_call" | custom-call | flops 20000000000 | bytes 1 | tf_op jit(solution)/shard_map/attend_back/pallas_call | solution.py:98
  264.1 4.5 %qkv_grads.1.refs_1_ = bf16[8,112,1024]{2,1,0:T(8,128)(2,1)S(1)} custom-call(s32[1]{0:T(128)} %bitcast.3.refs_0_, bf16[4,4,64,256]{3,2,1,0:T(8,128)(2,1)S(1)} %copy-done.22, bf16[4,4,64,512]{3,2,1,0:T(8,128)(2,1)S(1)} %add_split.12.refs_2_.refs_1_, bf16[256,1024]{1,0:T(8,128)(2,1)} %bitcast.2.refs_0_.refs_7_.refs_3_, bf16[256,1024]{1,0:T(8,128)(2,1)S(1)} %copy-done.21, ...), custom_call_target="tpu_custom_call" | custom-call | flops 1 | bytes 1 | tf_op jit(solution)/shard_map/qkv_grads/pallas_call | solution.py:98
  268.9 2.7 collective-permute-start.61
  272.2 2.1 collective-permute-start.48
  274.3 3.2 collective-permute-start.49
  277.5 24.5 %collective-permute-done.46.refs_0_ = bf16[4,4,64,512]{3,2,1,0:T(8,128)(2,1)S(1)} collective-permute-done((bf16[4,4,64,512]{3,2,1,0:T(8,128)(2,1)S(1)}, bf16[4,4,64,512]{3,2,1,0:T(8,128)(2,1)S(1)}, u32[]{:S(2)}, u32[]{:S(2)}) %collective-permute-start.46) | collective-permute-done | bytes 1048608 | tf_op jit(solution)/shard_map/ppermute | solution.py:35
  301.9 6.5 %collective-permute-done.48.refs_1_.refs_2_ = bf16[160,1024]{1,0:T(8,128)(2,1)S(1)} collective-permute-done((bf16[160,1024]{1,0:T(8,128)(2,1)S(1)}, bf16[160,1024]{1,0:T(8,128)(2,1)S(1)}, u32[]{:S(2)}, u32[]{:S(2)}) %collective-permute-start.48) | collective-permute-done | bytes 327712 | tf_op jit(solution)/shard_map/ppermute | solution.py:40
  309.7 1.9 dtokens.1
  313.5 2.1 collective-permute-start.52
  316.2 3.2 collective-permute-start.56
  319.4 7.9 %collective-permute-done.52.refs_1_ = bf16[256,1024]{1,0:T(8,128)(2,1)S(1)} collective-permute-done((bf16[256,1024]{1,0:T(8,128)(2,1)S(1)}, bf16[256,1024]{1,0:T(8,128)(2,1)S(1)}, u32[]{:S(2)}, u32[]{:S(2)}) %collective-permute-start.52) | collective-permute-done | bytes 524320 | tf_op jit(solution)/shard_map/ppermute | solution.py:35
  327.3 1.7 collective-permute-start.51
  331.0 6.6 %collective-permute-done.56.refs_4_ = bf16[144,1024]{1,0:T(8,128)(2,1)S(1)} collective-permute-done((bf16[144,1024]{1,0:T(8,128)(2,1)S(1)}, bf16[144,1024]{1,0:T(8,128)(2,1)S(1)}, u32[]{:S(2)}, u32[]{:S(2)}) %collective-permute-start.56) | collective-permute-done | bytes 294944 | tf_op jit(solution)/shard_map/ppermute | solution.py:40
  339.6 2.4 qkv_out.1
  342.6 7.6 %collective-permute-done.51.refs_2_ = bf16[256,1024]{1,0:T(8,128)(2,1)S(1)} collective-permute-done((bf16[256,1024]{1,0:T(8,128)(2,1)}, bf16[256,1024]{1,0:T(8,128)(2,1)S(1)}, u32[]{:S(2)}, u32[]{:S(2)}) %collective-permute-start.51) | collective-permute-done | bytes 524320 | tf_op jit(solution)/shard_map/ppermute | solution.py:35
  350.1 4.6 %collective-permute-done.53.refs_3_ = bf16[256,1024]{1,0:T(8,128)(2,1)S(1)} collective-permute-done((bf16[256,1024]{1,0:T(8,128)(2,1)}, bf16[256,1024]{1,0:T(8,128)(2,1)S(1)}, u32[]{:S(2)}, u32[]{:S(2)}) %collective-permute-start.53) | collective-permute-done | bytes 524320 | tf_op jit(solution)/shard_map/ppermute | solution.py:35
  355.7 2.1 all-gather.7.cloned.1.call-done
  357.9 4.7 %feed_out.1 = (f32[1024,1024]{1,0:T(8,128)}, f32[1024,1024]{1,0:T(8,128)}, f32[8,128]{1,0:T(8,128)}) custom-call(bf16[8,272,1024]{2,1,0:T(8,128)(2,1)} %bitcast.29), custom_call_target="tpu_custom_call" | custom-call | tf_op jit(solution)/shard_map/feed_out/pallas_call | solution.py:1020
  (346 shorter events, 67.6 us)
Async XLA Ops:
  7.2 107.9 %all-gather.5.cloned.1.call-start = ((), (), s32[]{:S(2)}) async-start(), calls=%async_computation | async-start | bytes 2162688 | tf_op jit(solution)/shard_map/all_gather | solution.py:1113
  8.7 349.1 %all-gather.7.cloned.1.call-start = ((), (), s32[]{:S(2)}) async-start(), calls=%async_computation.1 | async-start | bytes 5013504 | tf_op jit(solution)/shard_map/all_gather | solution.py:1318
  8.8 27.5 %collective-permute-start = (bf16[256,1024]{1,0:T(8,128)(2,1)}, bf16[256,1024]{1,0:T(8,128)(2,1)S(1)}, u32[]{:S(2)}, u32[]{:S(2)}) collective-permute-start(bf16[256,1024]{1,0:T(8,128)(2,1)} %bitcast.2.refs_0_.refs_7_.refs_3_), channel_id=1, source_target_pairs={{0,1},{1,0},{2,3},{3,2},{4,5},{5,4},{6,7},{7,6},{8,9},{9,8},{10,11... | collective-permute-start | bytes 1572872 | tf_op jit(solution)/shard_map/ppermute | solution.py:35
  11.9 27.0 %collective-permute-start.1 = (bf16[256,1024]{1,0:T(8,128)(2,1)}, bf16[256,1024]{1,0:T(8,128)(2,1)S(1)}, u32[]{:S(2)}, u32[]{:S(2)}) collective-permute-start(bf16[256,1024]{1,0:T(8,128)(2,1)} %bitcast.2.refs_0_.refs_7_.refs_3_), channel_id=1, source_target_pairs={{0,2},{1,3},{2,0},{3,1},{4,6},{5,7},{6,4},{7,5},{8,10},{9,11},{10,... | collective-permute-start | bytes 1572872 | tf_op jit(solution)/shard_map/ppermute | solution.py:35
  44.0 18.3 %collective-permute-start.9 = (bf16[3,4,64,512]{3,2,1,0:T(8,128)(2,1)}, bf16[3,4,64,512]{3,2,1,0:T(8,128)(2,1)}, u32[]{:S(2)}, u32[]{:S(2)}) collective-permute-start(bf16[3,4,64,512]{3,2,1,0:T(8,128)(2,1)} %get-tuple-element.112.refs_5_.refs_12_), channel_id=1, source_target_pairs={{0,8},{4,12},{8,0},{12,4},{1,9},{5,13},{9,1},{13,5},{2,10},{6,14},... | collective-permute-start | bytes 2359304 | tf_op jit(solution)/shard_map/ppermute | solution.py:35
  45.6 20.4 %collective-permute-start.2 = (bf16[256,1024]{1,0:T(8,128)(2,1)}, bf16[256,1024]{1,0:T(8,128)(2,1)}, u32[]{:S(2)}, u32[]{:S(2)}) collective-permute-start(bf16[256,1024]{1,0:T(8,128)(2,1)} %copy-done.50), channel_id=1, source_target_pairs={{0,1},{1,0},{2,3},{3,2},{4,5},{5,4},{6,7},{7,6},{8,9},{9,8},{10,11... | collective-permute-start | bytes 1572872 | tf_op jit(solution)/shard_map/ppermute | solution.py:35
  46.5 18.6 %collective-permute-start.3 = (bf16[1,144,1024]{2,1,0:T(8,128)(2,1)S(1)}, bf16[1,144,1024]{2,1,0:T(8,128)(2,1)S(1)}, u32[]{:S(2)}, u32[]{:S(2)}) collective-permute-start(bf16[1,144,1024]{2,1,0:T(8,128)(2,1)S(1)} %pack_inner.1), channel_id=1, source_target_pairs={{0,2},{1,3},{2,0},{3,1},{4,6},{5,7},{6,4},{7,5},{8,10},{9,11},{10,... | collective-permute-start | bytes 884744 | tf_op jit(solution)/shard_map/ppermute | solution.py:35
  49.4 43.5 %collective-permute-start.7 = (bf16[3,4,64,512]{3,2,1,0:T(8,128)(2,1)}, bf16[3,4,64,512]{3,2,1,0:T(8,128)(2,1)}, u32[]{:S(2)}, u32[]{:S(2)}) collective-permute-start(bf16[3,4,64,512]{3,2,1,0:T(8,128)(2,1)} %get-tuple-element.112.refs_5_.refs_12_), channel_id=1, source_target_pairs={{0,4},{4,0},{8,12},{12,8},{1,5},{5,1},{9,13},{13,9},{2,6},{6,2},{1... | collective-permute-start | bytes 2359304 | tf_op jit(solution)/shard_map/ppermute | solution.py:35
  62.3 30.7 %collective-permute-start.11 = (bf16[3,4,64,512]{3,2,1,0:T(8,128)(2,1)}, bf16[3,4,64,512]{3,2,1,0:T(8,128)(2,1)}, u32[]{:S(2)}, u32[]{:S(2)}) collective-permute-start(bf16[3,4,64,512]{3,2,1,0:T(8,128)(2,1)} %collective-permute-done.9.refs_9_.refs_16_), channel_id=1, source_target_pairs={{0,4},{4,0},{8,12},{12,8},{1,5},{5,1},{9,13},{13,9},{2,6},{6,2},{1... | collective-permute-start | bytes 2359304 | tf_op jit(solution)/shard_map/ppermute | solution.py:35
  65.2 19.2 %collective-permute-start.4 = (bf16[1,144,1024]{2,1,0:T(8,128)(2,1)S(1)}, bf16[1,144,1024]{2,1,0:T(8,128)(2,1)S(1)}, u32[]{:S(2)}, u32[]{:S(2)}) collective-permute-start(bf16[1,144,1024]{2,1,0:T(8,128)(2,1)S(1)} %collective-permute-done.3.refs_0_), channel_id=1, source_target_pairs={{0,8},{4,12},{8,0},{12,4},{1,9},{5,13},{9,1},{13,5},{2,10},{6,14},... | collective-permute-start | bytes 884744 | tf_op jit(solution)/shard_map/ppermute | solution.py:35
  66.0 16.8 %collective-permute-start.5 = (bf16[1,128,1024]{2,1,0:T(8,128)(2,1)S(1)}, bf16[1,128,1024]{2,1,0:T(8,128)(2,1)S(1)}, u32[]{:S(2)}, u32[]{:S(2)}) collective-permute-start(bf16[1,128,1024]{2,1,0:T(8,128)(2,1)S(1)} %pack_outer.1), channel_id=1, source_target_pairs={{0,2},{1,3},{2,0},{3,1},{4,6},{5,7},{6,4},{7,5},{8,10},{9,11},{10,... | collective-permute-start | bytes 786440 | tf_op jit(solution)/shard_map/ppermute | solution.py:35
  72.2 12.2 %collective-permute-start.10 = (bf16[1,4,64,512]{3,2,1,0:T(8,128)(2,1)}, bf16[1,4,64,512]{3,2,1,0:T(8,128)(2,1)S(1)}, u32[]{:S(2)}, u32[]{:S(2)}) collective-permute-start(bf16[1,4,64,512]{3,2,1,0:T(8,128)(2,1)} %get-tuple-element.113.refs_6_.refs_13_), channel_id=1, source_target_pairs={{0,8},{4,12},{8,0},{12,4},{1,9},{5,13},{9,1},{13,5},{2,10},{6,14},... | collective-permute-start | bytes 786440 | tf_op jit(solution)/shard_map/ppermute | solution.py:35
  82.8 7.1 %collective-permute-start.6 = (bf16[1,128,1024]{2,1,0:T(8,128)(2,1)S(1)}, bf16[1,128,1024]{2,1,0:T(8,128)(2,1)S(1)}, u32[]{:S(2)}, u32[]{:S(2)}) collective-permute-start(bf16[1,128,1024]{2,1,0:T(8,128)(2,1)S(1)} %collective-permute-done.5.refs_2_), channel_id=1, source_target_pairs={{0,16},{16,0},{1,17},{17,1},{2,18},{18,2},{3,19},{19,3},{4,20},{20... | collective-permute-start | bytes 786440 | tf_op jit(solution)/shard_map/ppermute | solution.py:35
  84.3 8.6 %collective-permute-start.8 = (bf16[1,4,64,512]{3,2,1,0:T(8,128)(2,1)}, bf16[1,4,64,512]{3,2,1,0:T(8,128)(2,1)S(1)}, u32[]{:S(2)}, u32[]{:S(2)}) collective-permute-start(bf16[1,4,64,512]{3,2,1,0:T(8,128)(2,1)} %get-tuple-element.113.refs_6_.refs_13_), channel_id=1, source_target_pairs={{0,4},{4,0},{8,12},{12,8},{1,5},{5,1},{9,13},{13,9},{2,6},{6,2},{1... | collective-permute-start | bytes 786440 | tf_op jit(solution)/shard_map/ppermute | solution.py:35
  84.4 8.6 %collective-permute-start.12 = (bf16[1,4,64,512]{3,2,1,0:T(8,128)(2,1)S(1)}, bf16[1,4,64,512]{3,2,1,0:T(8,128)(2,1)S(1)}, u32[]{:S(2)}, u32[]{:S(2)}) collective-permute-start(bf16[1,4,64,512]{3,2,1,0:T(8,128)(2,1)S(1)} %collective-permute-done.10.refs_10_.refs_17_), channel_id=1, source_target_pairs={{0,4},{4,0},{8,12},{12,8},{1,5},{5,1},{9,13},{13,9},{2,6},{6,2},{1... | collective-permute-start | bytes 786440 | tf_op jit(solution)/shard_map/ppermute | solution.py:35
  103.4 7.9 %collective-permute-start.13 = (bf16[256,256]{1,0:T(8,128)(2,1)}, bf16[256,256]{1,0:T(8,128)(2,1)S(1)}, u32[]{:S(2)}, u32[]{:S(2)}) collective-permute-start(bf16[256,256]{1,0:T(8,128)(2,1)} %bitcast.44), channel_id=1, source_target_pairs={{0,1},{1,0},{2,3},{3,2},{4,5},{5,4},{6,7},{7,6},{8,9},{9,8},{10,11... | collective-permute-start | bytes 393224 | tf_op jit(solution)/shard_map/ppermute | solution.py:35
  103.5 11.6 %collective-permute-start.14 = (bf16[256,256]{1,0:T(8,128)(2,1)}, bf16[256,256]{1,0:T(8,128)(2,1)S(1)}, u32[]{:S(2)}, u32[]{:S(2)}) collective-permute-start(bf16[256,256]{1,0:T(8,128)(2,1)} %bitcast.43), channel_id=1, source_target_pairs={{0,2},{1,3},{2,0},{3,1},{4,6},{5,7},{6,4},{7,5},{8,10},{9,11},{10,... | collective-permute-start | bytes 393224 | tf_op jit(solution)/shard_map/ppermute | solution.py:35
  105.1 10.0 %collective-permute-start.15 = (bf16[256,256]{1,0:T(8,128)(2,1)}, bf16[256,256]{1,0:T(8,128)(2,1)S(1)}, u32[]{:S(2)}, u32[]{:S(2)}) collective-permute-start(bf16[256,256]{1,0:T(8,128)(2,1)} %bitcast.42), channel_id=1, source_target_pairs={{0,3},{1,2},{2,1},{3,0},{4,7},{5,6},{6,5},{7,4},{8,11},{9,10},{10,... | collective-permute-start | bytes 393224 | tf_op jit(solution)/shard_map/ppermute | solution.py:35
  107.8 19.0 %collective-permute-start.17 = (bf16[2,144,1024]{2,1,0:T(8,128)(2,1)S(1)}, bf16[2,144,1024]{2,1,0:T(8,128)(2,1)S(1)}, u32[]{:S(2)}, u32[]{:S(2)}) collective-permute-start(bf16[2,144,1024]{2,1,0:T(8,128)(2,1)S(1)} %copy-done.92), channel_id=1, source_target_pairs={{0,16},{16,0},{1,17},{17,1},{2,18},{18,2},{3,19},{19,3},{4,20},{20... | collective-permute-start | bytes 1769480 | tf_op jit(solution)/shard_map/ppermute | solution.py:35
  108.6 18.2 %collective-permute-start.18 = (bf16[2,128,1024]{2,1,0:T(8,128)(2,1)}, bf16[2,128,1024]{2,1,0:T(8,128)(2,1)}, u32[]{:S(2)}, u32[]{:S(2)}) collective-permute-start(bf16[2,128,1024]{2,1,0:T(8,128)(2,1)} %get-tuple-element.111.refs_4_.refs_5_), channel_id=1, source_target_pairs={{0,8},{4,12},{8,0},{12,4},{1,9},{5,13},{9,1},{13,5},{2,10},{6,14},... | collective-permute-start | bytes 1572872 | tf_op jit(solution)/shard_map/ppermute | solution.py:35
  121.1 11.0 %collective-permute-start.16 = (bf16[256,1024]{1,0:T(8,128)(2,1)}, bf16[256,1024]{1,0:T(8,128)(2,1)S(1)}, u32[]{:S(2)}, u32[]{:S(2)}) collective-permute-start(bf16[256,1024]{1,0:T(8,128)(2,1)} %get-tuple-element.119.refs_7_.refs_0_.refs_2_), channel_id=1, source_target_pairs={{0,4},{4,0},{8,12},{12,8},{1,5},{5,1},{9,13},{13,9},{2,6},{6,2},{1... | collective-permute-start | bytes 1572872 | tf_op jit(solution)/shard_map/ppermute | solution.py:35
  121.2 20.0 %collective-permute-start.21 = (bf16[256,1024]{1,0:T(8,128)(2,1)S(1)}, bf16[256,1024]{1,0:T(8,128)(2,1)}, u32[]{:S(2)}, u32[]{:S(2)}) collective-permute-start(bf16[256,1024]{1,0:T(8,128)(2,1)S(1)} %copy-done.20), channel_id=1, source_target_pairs={{0,8},{4,12},{8,0},{12,4},{1,9},{5,13},{9,1},{13,5},{2,10},{6,14},... | collective-permute-start | bytes 1572872 | tf_op jit(solution)/shard_map/ppermute | solution.py:35
  124.8 16.5 %collective-permute-start.20 = (bf16[256,1024]{1,0:T(8,128)(2,1)}, bf16[256,1024]{1,0:T(8,128)(2,1)}, u32[]{:S(2)}, u32[]{:S(2)}) collective-permute-start(bf16[256,1024]{1,0:T(8,128)(2,1)} %get-tuple-element.119.refs_7_.refs_0_.refs_2_), channel_id=1, source_target_pairs={{0,1},{1,0},{2,3},{3,2},{4,5},{5,4},{6,7},{7,6},{8,9},{9,8},{10,11... | collective-permute-start | bytes 1572872 | tf_op jit(solution)/shard_map/ppermute | solution.py:35
  142.9 2.0 collective-permute-start.22
  149.8 1.9 collective-permute-start.23
  149.9 14.2 %collective-permute-start.25 = (bf16[256,1024]{1,0:T(8,128)(2,1)S(1)}, bf16[256,1024]{1,0:T(8,128)(2,1)S(1)}, u32[]{:S(2)}, u32[]{:S(2)}) collective-permute-start(bf16[256,1024]{1,0:T(8,128)(2,1)S(1)} %collective-permute-done.1.refs_0_.refs_5_), channel_id=1, source_target_pairs={{0,8},{4,12},{8,0},{12,4},{1,9},{5,13},{9,1},{13,5},{2,10},{6,14},... | collective-permute-start | bytes 1572872 | tf_op jit(solution)/shard_map/ppermute | solution.py:35
  150.0 14.1 %collective-permute-start.19 = (bf16[256,1024]{1,0:T(8,128)(2,1)}, bf16[256,1024]{1,0:T(8,128)(2,1)}, u32[]{:S(2)}, u32[]{:S(2)}) collective-permute-start(bf16[256,1024]{1,0:T(8,128)(2,1)} %get-tuple-element.124), channel_id=1, source_target_pairs={{0,4},{4,0},{8,12},{12,8},{1,5},{5,1},{9,13},{13,9},{2,6},{6,2},{1... | collective-permute-start | bytes 1572872 | tf_op jit(solution)/shard_map/ppermute | solution.py:35
  152.6 14.3 %collective-permute-start.24 = (bf16[256,1024]{1,0:T(8,128)(2,1)}, bf16[256,1024]{1,0:T(8,128)(2,1)}, u32[]{:S(2)}, u32[]{:S(2)}) collective-permute-start(bf16[256,1024]{1,0:T(8,128)(2,1)} %add_split.8), channel_id=1, source_target_pairs={{0,1},{1,0},{2,3},{3,2},{4,5},{5,4},{6,7},{7,6},{8,9},{9,8},{10,11... | collective-permute-start | bytes 1572872 | tf_op jit(solution)/shard_map/ppermute | solution.py:35
  174.5 1.9 collective-permute-start.26
  174.5 14.5 %collective-permute-start.29 = (bf16[256,1024]{1,0:T(8,128)(2,1)}, bf16[256,1024]{1,0:T(8,128)(2,1)S(1)}, u32[]{:S(2)}, u32[]{:S(2)}) collective-permute-start(bf16[256,1024]{1,0:T(8,128)(2,1)} %collective-permute-done.2.refs_0_.refs_1_.refs_6_), channel_id=1, source_target_pairs={{0,8},{4,12},{8,0},{12,4},{1,9},{5,13},{9,1},{13,5},{2,10},{6,14},... | collective-permute-start | bytes 1572872 | tf_op jit(solution)/shard_map/ppermute | solution.py:35
  175.1 14.1 %collective-permute-start.28 = (bf16[256,1024]{1,0:T(8,128)(2,1)S(1)}, bf16[256,1024]{1,0:T(8,128)(2,1)S(1)}, u32[]{:S(2)}, u32[]{:S(2)}) collective-permute-start(bf16[256,1024]{1,0:T(8,128)(2,1)S(1)} %get-tuple-element.130.refs_0_.refs_2_), channel_id=1, source_target_pairs={{0,1},{1,0},{2,3},{3,2},{4,5},{5,4},{6,7},{7,6},{8,9},{9,8},{10,11... | collective-permute-start | bytes 1572872 | tf_op jit(solution)/shard_map/ppermute | solution.py:35
  189.2 2.0 collective-permute-start.30
  194.8 1.9 collective-permute-start.31
  194.9 14.5 %collective-permute-start.33 = (bf16[256,1024]{1,0:T(8,128)(2,1)}, bf16[256,1024]{1,0:T(8,128)(2,1)}, u32[]{:S(2)}, u32[]{:S(2)}) collective-permute-start(bf16[256,1024]{1,0:T(8,128)(2,1)} %bitcast.2.refs_0_.refs_7_.refs_3_), channel_id=1, source_target_pairs={{0,8},{4,12},{8,0},{12,4},{1,9},{5,13},{9,1},{13,5},{2,10},{6,14},... | collective-permute-start | bytes 1572872 | tf_op jit(solution)/shard_map/ppermute | solution.py:35
  196.3 13.1 %collective-permute-start.27 = (bf16[256,1024]{1,0:T(8,128)(2,1)}, bf16[256,1024]{1,0:T(8,128)(2,1)}, u32[]{:S(2)}, u32[]{:S(2)}) collective-permute-start(bf16[256,1024]{1,0:T(8,128)(2,1)} %get-tuple-element.133), channel_id=1, source_target_pairs={{0,4},{4,0},{8,12},{12,8},{1,5},{5,1},{9,13},{13,9},{2,6},{6,2},{1... | collective-permute-start | bytes 1572872 | tf_op jit(solution)/shard_map/ppermute | solution.py:35
  196.8 14.1 %collective-permute-start.32 = (bf16[256,1024]{1,0:T(8,128)(2,1)S(1)}, bf16[256,1024]{1,0:T(8,128)(2,1)}, u32[]{:S(2)}, u32[]{:S(2)}) collective-permute-start(bf16[256,1024]{1,0:T(8,128)(2,1)S(1)} %add_split.9.refs_6_), channel_id=1, source_target_pairs={{0,1},{1,0},{2,3},{3,2},{4,5},{5,4},{6,7},{7,6},{8,9},{9,8},{10,11... | collective-permute-start | bytes 1572872 | tf_op jit(solution)/shard_map/ppermute | solution.py:35
  215.0 3.7 %collective-permute-start.38 = (bf16[528,1024]{1,0:T(8,128)(2,1)S(1)}, bf16[528,1024]{1,0:T(8,128)(2,1)S(1)}, u32[]{:S(2)}, u32[]{:S(2)}) collective-permute-start(bf16[528,1024]{1,0:T(8,128)(2,1)S(1)} %get-tuple-element.154), channel_id=1, source_target_pairs={{0,4},{4,0},{8,12},{12,8},{1,5},{5,1},{9,13},{13,9},{2,6},{6,2},{1... | collective-permute-start | bytes 3244040 | tf_op jit(solution)/shard_map/ppermute | solution.py:35
  215.0 27.0 %collective-permute-start.40 = (bf16[2,272,1024]{2,1,0:T(8,128)(2,1)S(1)}, bf16[2,272,1024]{2,1,0:T(8,128)(2,1)S(1)}, u32[]{:S(2)}, u32[]{:S(2)}) collective-permute-start(bf16[2,272,1024]{2,1,0:T(8,128)(2,1)S(1)} %weight_grad.4.refs_9_), channel_id=1, source_target_pairs={{0,8},{4,12},{8,0},{12,4},{1,9},{5,13},{9,1},{13,5},{2,10},{6,14},... | collective-permute-start | bytes 3342344 | tf_op jit(solution)/shard_map/ppermute | solution.py:35
  217.8 25.3 %collective-permute-start.37 = (bf16[2,256,1024]{2,1,0:T(8,128)(2,1)S(1)}, bf16[2,256,1024]{2,1,0:T(8,128)(2,1)S(1)}, u32[]{:S(2)}, u32[]{:S(2)}) collective-permute-start(bf16[2,256,1024]{2,1,0:T(8,128)(2,1)S(1)} %weight_grad.6), channel_id=1, source_target_pairs={{0,16},{16,0},{1,17},{17,1},{2,18},{18,2},{3,19},{19,3},{4,20},{20... | collective-permute-start | bytes 3145736 | tf_op jit(solution)/shard_map/ppermute | solution.py:35
  219.0 18.4 %collective-permute-start.39 = (bf16[272,1024]{1,0:T(8,128)(2,1)S(1)}, bf16[272,1024]{1,0:T(8,128)(2,1)S(1)}, u32[]{:S(2)}, u32[]{:S(2)}) collective-permute-start(bf16[272,1024]{1,0:T(8,128)(2,1)S(1)} %get-tuple-element.156), channel_id=1, source_target_pairs={{0,1},{1,0},{2,3},{3,2},{4,5},{5,4},{6,7},{7,6},{8,9},{9,8},{10,11... | collective-permute-start | bytes 1671176 | tf_op jit(solution)/shard_map/ppermute | solution.py:35
  219.4 25.7 %collective-permute-start.34 = (bf16[256,256]{1,0:T(8,128)(2,1)S(1)}, bf16[256,256]{1,0:T(8,128)(2,1)S(1)}, u32[]{:S(2)}, u32[]{:S(2)}) collective-permute-start(bf16[256,256]{1,0:T(8,128)(2,1)S(1)} %get-tuple-element.144), channel_id=1, source_target_pairs={{0,1},{1,0},{2,3},{3,2},{4,5},{5,4},{6,7},{7,6},{8,9},{9,8},{10,11... | collective-permute-start | bytes 393224 | tf_op jit(solution)/shard_map/ppermute | solution.py:35
  221.1 24.9 %collective-permute-start.35 = (bf16[256,256]{1,0:T(8,128)(2,1)S(1)}, bf16[256,256]{1,0:T(8,128)(2,1)S(1)}, u32[]{:S(2)}, u32[]{:S(2)}) collective-permute-start(bf16[256,256]{1,0:T(8,128)(2,1)S(1)} %get-tuple-element.145), channel_id=1, source_target_pairs={{0,2},{1,3},{2,0},{3,1},{4,6},{5,7},{6,4},{7,5},{8,10},{9,11},{10,... | collective-permute-start | bytes 393224 | tf_op jit(solution)/shard_map/ppermute | solution.py:35
  237.4 8.6 %collective-permute-start.36 = (bf16[256,256]{1,0:T(8,128)(2,1)S(1)}, bf16[256,256]{1,0:T(8,128)(2,1)S(1)}, u32[]{:S(2)}, u32[]{:S(2)}) collective-permute-start(bf16[256,256]{1,0:T(8,128)(2,1)S(1)} %get-tuple-element.146), channel_id=1, source_target_pairs={{0,3},{1,2},{2,1},{3,0},{4,7},{5,6},{6,5},{7,4},{8,11},{9,10},{10,... | collective-permute-start | bytes 393224 | tf_op jit(solution)/shard_map/ppermute | solution.py:35
  242.0 17.3 %collective-permute-start.43 = (bf16[144,1024]{1,0:T(8,128)(2,1)S(1)}, bf16[144,1024]{1,0:T(8,128)(2,1)S(1)}, u32[]{:S(2)}, u32[]{:S(2)}) collective-permute-start(bf16[144,1024]{1,0:T(8,128)(2,1)S(1)} %get-tuple-element.158.refs_2_.refs_11_), channel_id=1, source_target_pairs={{0,2},{1,3},{2,0},{3,1},{4,6},{5,7},{6,4},{7,5},{8,10},{9,11},{10,... | collective-permute-start | bytes 884744 | tf_op jit(solution)/shard_map/ppermute | solution.py:35
  243.1 16.3 %collective-permute-start.41 = (bf16[1,272,1024]{2,1,0:T(8,128)(2,1)S(1)}, bf16[1,272,1024]{2,1,0:T(8,128)(2,1)S(1)}, u32[]{:S(2)}, u32[]{:S(2)}) collective-permute-start(bf16[1,272,1024]{2,1,0:T(8,128)(2,1)S(1)} %get-tuple-element.165), channel_id=1, source_target_pairs={{0,16},{16,0},{1,17},{17,1},{2,18},{18,2},{3,19},{19,3},{4,20},{20... | collective-permute-start | bytes 1671176 | tf_op jit(solution)/shard_map/ppermute | solution.py:35
  245.1 14.3 %collective-permute-start.42 = (bf16[1,256,1024]{2,1,0:T(8,128)(2,1)S(1)}, bf16[1,256,1024]{2,1,0:T(8,128)(2,1)S(1)}, u32[]{:S(2)}, u32[]{:S(2)}) collective-permute-start(bf16[1,256,1024]{2,1,0:T(8,128)(2,1)S(1)} %get-tuple-element.166), channel_id=1, source_target_pairs={{0,8},{4,12},{8,0},{12,4},{1,9},{5,13},{9,1},{13,5},{2,10},{6,14},... | collective-permute-start | bytes 1572872 | tf_op jit(solution)/shard_map/ppermute | solution.py:35
  259.4 2.9 collective-permute-start.44
  259.5 4.4 %collective-permute-start.45 = (bf16[4,4,64,512]{3,2,1,0:T(8,128)(2,1)}, bf16[4,4,64,512]{3,2,1,0:T(8,128)(2,1)S(1)}, u32[]{:S(2)}, u32[]{:S(2)}) collective-permute-start(bf16[4,4,64,512]{3,2,1,0:T(8,128)(2,1)} %get-tuple-element.169), channel_id=1, source_target_pairs={{0,4},{4,0},{8,12},{12,8},{1,5},{5,1},{9,13},{13,9},{2,6},{6,2},{1... | collective-permute-start | bytes 3145736 | tf_op jit(solution)/shard_map/ppermute | solution.py:35
  268.7 2.9 collective-permute-start.47
  268.9 33.0 %collective-permute-start.46 = (bf16[4,4,64,512]{3,2,1,0:T(8,128)(2,1)S(1)}, bf16[4,4,64,512]{3,2,1,0:T(8,128)(2,1)S(1)}, u32[]{:S(2)}, u32[]{:S(2)}) collective-permute-start(bf16[4,4,64,512]{3,2,1,0:T(8,128)(2,1)S(1)} %add_split.13.refs_7_), channel_id=1, source_target_pairs={{0,8},{4,12},{8,0},{12,4},{1,9},{5,13},{9,1},{13,5},{2,10},{6,14},... | collective-permute-start | bytes 3145736 | tf_op jit(solution)/shard_map/ppermute | solution.py:35
  268.9 43.6 %collective-permute-start.61 = (bf16[272,1024]{1,0:T(8,128)(2,1)S(1)}, bf16[272,1024]{1,0:T(8,128)(2,1)S(1)}, u32[]{:S(2)}, u32[]{:S(2)}) collective-permute-start(bf16[272,1024]{1,0:T(8,128)(2,1)S(1)} %get-tuple-element.170.refs_12_), channel_id=1, source_target_pairs={{0,2},{1,3},{2,0},{3,1},{4,6},{5,7},{6,4},{7,5},{8,10},{9,11},{10,... | collective-permute-start | bytes 1671176 | tf_op jit(solution)/shard_map/ppermute | solution.py:35
  272.2 36.2 %collective-permute-start.48 = (bf16[160,1024]{1,0:T(8,128)(2,1)S(1)}, bf16[160,1024]{1,0:T(8,128)(2,1)S(1)}, u32[]{:S(2)}, u32[]{:S(2)}) collective-permute-start(bf16[160,1024]{1,0:T(8,128)(2,1)S(1)} %get-tuple-element.173), channel_id=1, source_target_pairs={{0,8},{4,12},{8,0},{12,4},{16,24},{20,28},{24,16},{28,20},{1,9},{5... | collective-permute-start | bytes 983048 | tf_op jit(solution)/shard_map/ppermute | solution.py:40
  274.3 34.1 %collective-permute-start.49 = (bf16[160,1024]{1,0:T(8,128)(2,1)S(1)}, bf16[160,1024]{1,0:T(8,128)(2,1)S(1)}, u32[]{:S(2)}, u32[]{:S(2)}) collective-permute-start(bf16[160,1024]{1,0:T(8,128)(2,1)S(1)} %get-tuple-element.174), channel_id=1, source_target_pairs={{0,16},{4,20},{8,24},{12,28},{16,0},{20,4},{24,8},{28,12},{1,17},{... | collective-permute-start | bytes 983048 | tf_op jit(solution)/shard_map/ppermute | solution.py:40
  277.5 30.9 %collective-permute-start.50 = (bf16[160,1024]{1,0:T(8,128)(2,1)S(1)}, bf16[160,1024]{1,0:T(8,128)(2,1)S(1)}, u32[]{:S(2)}, u32[]{:S(2)}) collective-permute-start(bf16[160,1024]{1,0:T(8,128)(2,1)S(1)} %get-tuple-element.175), channel_id=1, source_target_pairs={{0,24},{4,28},{8,16},{12,20},{16,8},{20,12},{24,0},{28,4},{1,25},{... | collective-permute-start | bytes 983048 | tf_op jit(solution)/shard_map/ppermute | solution.py:40
  313.5 13.8 %collective-permute-start.52 = (bf16[256,1024]{1,0:T(8,128)(2,1)S(1)}, bf16[256,1024]{1,0:T(8,128)(2,1)S(1)}, u32[]{:S(2)}, u32[]{:S(2)}) collective-permute-start(bf16[256,1024]{1,0:T(8,128)(2,1)S(1)} %get-tuple-element.180.refs_5_.refs_2_), channel_id=1, source_target_pairs={{0,1},{1,0},{2,3},{3,2},{4,5},{5,4},{6,7},{7,6},{8,9},{9,8},{10,11... | collective-permute-start | bytes 1572872 | tf_op jit(solution)/shard_map/ppermute | solution.py:35
  315.8 14.1 %collective-permute-start.54 = (bf16[144,1024]{1,0:T(8,128)(2,1)S(1)}, bf16[144,1024]{1,0:T(8,128)(2,1)S(1)}, u32[]{:S(2)}, u32[]{:S(2)}) collective-permute-start(bf16[144,1024]{1,0:T(8,128)(2,1)S(1)} %get-tuple-element.182.refs_2_.refs_1_), channel_id=1, source_target_pairs={{0,8},{4,12},{8,0},{12,4},{16,24},{20,28},{24,16},{28,20},{1,9},{5... | collective-permute-start | bytes 884744 | tf_op jit(solution)/shard_map/ppermute | solution.py:40
  316.2 14.8 %collective-permute-start.55 = (bf16[144,1024]{1,0:T(8,128)(2,1)S(1)}, bf16[144,1024]{1,0:T(8,128)(2,1)S(1)}, u32[]{:S(2)}, u32[]{:S(2)}) collective-permute-start(bf16[144,1024]{1,0:T(8,128)(2,1)S(1)} %get-tuple-element.182.refs_2_.refs_1_), channel_id=1, source_target_pairs={{0,16},{4,20},{8,24},{12,28},{16,0},{20,4},{24,8},{28,12},{1,17},{... | collective-permute-start | bytes 884744 | tf_op jit(solution)/shard_map/ppermute | solution.py:40
  316.2 21.4 %collective-permute-start.56 = (bf16[144,1024]{1,0:T(8,128)(2,1)S(1)}, bf16[144,1024]{1,0:T(8,128)(2,1)S(1)}, u32[]{:S(2)}, u32[]{:S(2)}) collective-permute-start(bf16[144,1024]{1,0:T(8,128)(2,1)S(1)} %get-tuple-element.182.refs_2_.refs_1_), channel_id=1, source_target_pairs={{0,24},{4,28},{8,16},{12,20},{16,8},{20,12},{24,0},{28,4},{1,25},{... | collective-permute-start | bytes 884744 | tf_op jit(solution)/shard_map/ppermute | solution.py:40
  319.4 18.2 %collective-permute-start.57 = (bf16[144,1024]{1,0:T(8,128)(2,1)S(1)}, bf16[144,1024]{1,0:T(8,128)(2,1)S(1)}, u32[]{:S(2)}, u32[]{:S(2)}) collective-permute-start(bf16[144,1024]{1,0:T(8,128)(2,1)S(1)} %get-tuple-element.182.refs_2_.refs_1_), channel_id=1, source_target_pairs={{0,4},{4,0},{8,12},{12,8},{1,5},{5,1},{9,13},{13,9},{2,6},{6,2},{1... | collective-permute-start | bytes 884744 | tf_op jit(solution)/shard_map/ppermute | solution.py:35
  327.3 22.9 %collective-permute-start.51 = (bf16[256,1024]{1,0:T(8,128)(2,1)}, bf16[256,1024]{1,0:T(8,128)(2,1)S(1)}, u32[]{:S(2)}, u32[]{:S(2)}) collective-permute-start(bf16[256,1024]{1,0:T(8,128)(2,1)} %get-tuple-element.178), channel_id=1, source_target_pairs={{0,1},{1,0},{2,3},{3,2},{4,5},{5,4},{6,7},{7,6},{8,9},{9,8},{10,11... | collective-permute-start | bytes 1572872 | tf_op jit(solution)/shard_map/ppermute | solution.py:35
  330.0 24.8 %collective-permute-start.53 = (bf16[256,1024]{1,0:T(8,128)(2,1)}, bf16[256,1024]{1,0:T(8,128)(2,1)S(1)}, u32[]{:S(2)}, u32[]{:S(2)}) collective-permute-start(bf16[256,1024]{1,0:T(8,128)(2,1)} %add_split.14), channel_id=1, source_target_pairs={{0,2},{1,3},{2,0},{3,1},{4,6},{5,7},{6,4},{7,5},{8,10},{9,11},{10,... | collective-permute-start | bytes 1572872 | tf_op jit(solution)/shard_map/ppermute | solution.py:35
  331.0 7.7 %collective-permute-start.58 = (bf16[144,1024]{1,0:T(8,128)(2,1)S(1)}, bf16[144,1024]{1,0:T(8,128)(2,1)S(1)}, u32[]{:S(2)}, u32[]{:S(2)}) collective-permute-start(bf16[144,1024]{1,0:T(8,128)(2,1)S(1)} %collective-permute-done.54.refs_2_), channel_id=1, source_target_pairs={{0,4},{4,0},{8,12},{12,8},{1,5},{5,1},{9,13},{13,9},{2,6},{6,2},{1... | collective-permute-start | bytes 884744 | tf_op jit(solution)/shard_map/ppermute | solution.py:35
  337.5 1.6 collective-permute-start.59
  337.6 2.0 collective-permute-start.60
  (107 other events, 740.2 us)
Sparse Core Ops, SparseCore 0:
  11.6 76.7 all-gather.4
  313.6 44.2 all-gather.6
where the time goes:
time: 377 us; the launch traced here: 370 us
  waiting for transfers between devices  166 us (44%)
  Pallas kernels  87.3 us (23%)
  starting transfers between devices  60.9 us (16%)
  local copies, waits for them, and re-layouts  39.3 us (10%)
  between operations  16 us (4%)
    ppermute x56, waiting for transfers between devices, swap(): return lax.ppermute(value, axis, [(i, i ^ stride) for i in range(size)])  151 us
    pallas_call x41, Pallas kernels, kernel_call(): pl.pallas_call(whole, in_specs=[in_smem] * ns + [in_hbm if i in far_in el...  82.6 us
    ppermute x56, starting transfers between devices, swap(): return lax.ppermute(value, axis, [(i, i ^ stride) for i in range(size)])  52 us
    unnamed x214, local copies, waits for them, and re-layouts  30.3 us
    ppermute x6, waiting for transfers between devices, swap_slots(): lax.ppermute(value, ('dp', 'seq'), [(i, i ^ mask) for i in range(size)])  13 us
    ppermute x6, starting transfers between devices, swap_slots(): lax.ppermute(value, ('dp', 'seq'), [(i, i ^ mask) for i in range(size)])  8.82 us
  transfers between devices with their start and end apart: 64, of which 33 were waited for; matrix products, arithmetic and copies ran while one was open for 2% of the time, Pallas kernels for 17%

commit v1 on v0

--- a/solution.py
+++ b/solution.py
@@ -62,7 +62,7 @@
 
 
 def kernel_call(
-    body, name, arrays, out, scalars=(), scratch=(), mebibytes=16, waits=(), far_in=(), local=(), flops=1
+    body, name, arrays, out, scalars=(), scratch=(), mebibytes=16, waits=(), far_in=(), local=(), flops=1, early=None
 ):
     ns, na, nw, no, nl = len(scalars), len(arrays), len(waits), len(out), len(local)
     alone = name in kernels_alone
@@ -83,6 +83,8 @@
             copies.append(pltpu.make_async_copy(here[ns + i], held_refs[k], sems.at[k]))
             copies[-1].start()
             here[ns + i] = held_refs[k]
+        if early is not None:
+            early(*here, *kept, *outs, *rest)
         for copy in copies:
             copy.wait()
         copies = []
@@ -174,7 +176,7 @@
     return jnp.concatenate(found) * jnp.asarray(score_scale, low)
 
 
-def attend_kernel(counts, pos, *refs):
+def attend_kernel(counts, start, pos, *refs):
     stacks, arrays, groups = counts
     q_refs, kv_refs = refs[:stacks], refs[stacks : stacks + arrays]
     ctx_refs, (ctx_t_ref, lse_ref, kv_all, sems) = refs[stacks + arrays : -4], refs[-4:]
@@ -188,8 +190,10 @@
         start_keys(pos, p, proteins, groups, kv_refs, kv_all, sems, blocks, block, wait)
         return blocks
 
-    for p in range(proteins):
-        keys_of(p, False)
+    if start:
+        for p in range(proteins):
+            keys_of(p, False)
+        return
 
     def protein(p, carry):
         length = pos[p]
@@ -241,7 +245,7 @@
     lax.fori_loop(0, proteins, protein, 0)
 
 
-def attend_back_kernel(counts, pos, *refs):
+def attend_back_kernel(counts, start, pos, *refs):
     stacks, arrays, groups = counts
     q_refs, dctx_refs, refs = refs[:stacks], refs[stacks : stacks + groups], refs[stacks + groups :]
     ctx_t_ref, lse_ref, kv_refs, refs = refs[0], refs[1], refs[2 : 2 + arrays], refs[2 + arrays :]
@@ -257,8 +261,10 @@
         start_keys(pos, p, proteins, groups, kv_refs, kv_all, sems, blocks, block, wait)
         return blocks
 
-    for p in range(proteins):
-        keys_of(p, False)
+    if start:
+        for p in range(proteins):
+            keys_of(p, False)
+        return
 
     def results_of(p, wait):
         for j in range(groups):
@@ -327,7 +333,7 @@
     rows = groups * share
     total = share * sum(piece.shape[0] for piece in kv_pieces)
     found = kernel_call(
-        functools.partial(attend_kernel, (len(queries), len(kv_pieces), groups)),
+        functools.partial(attend_kernel, (len(queries), len(kv_pieces), groups), False),
         "attend",
         queries,
         [((proteins, share, width), low, hbm)] * groups
@@ -342,6 +348,7 @@
         local=kv_pieces,
         waits=waits,
         flops=int(1e10),
+        early=functools.partial(attend_kernel, (len(queries), len(kv_pieces), groups), True),
     )
     return found[:groups], found[groups], found[groups + 1]
 
@@ -353,7 +360,7 @@
     pieces = total // (groups * share)
     arrays = [*queries, *dctx, ctx_t, lse]
     found = kernel_call(
-        functools.partial(attend_back_kernel, (len(queries), len(kv_pieces), groups)),
+        functools.partial(attend_back_kernel, (len(queries), len(kv_pieces), groups), False),
         "attend_back",
         arrays,
         [((groups, proteins, share, width), low, "kernel")]
@@ -371,6 +378,7 @@
         local=kv_pieces,
         waits=waits,
         flops=int(2e10),
+        early=functools.partial(attend_back_kernel, (len(queries), len(kv_pieces), groups), True),
     )
     return found[0], found[1:]
 

time: 377 us -> 379 us (level)
  starting transfers between devices: 60.9 us -> 70.2 us
  waiting for transfers between devices: 166 us -> 159 us
    ppermute x56, starting transfers between devices: 52 us -> 63 us  [swap(): return lax.ppermute(value, axis, [(i, i ^ stride) for i in range(size)])]
    ppermute x56, waiting for transfers between devices: 151 us -> 146 us  [swap(): return lax.ppermute(value, axis, [(i, i ^ stride) for i in range(size)])]
  transfers between devices with their start and end apart: 64 -> 64, of which waited for: 33 -> 32; matrix products, arithmetic and copies ran while one was open for 2% -> 2% of each run, Pallas kernels for 17% -> 17%
where the time goes in v1:
time: 379 us; the launch traced here: 372 us
  waiting for transfers between devices  159 us (42%)
  Pallas kernels  87.1 us (23%)
  starting transfers between devices  70.2 us (19%)
  local copies, waits for them, and re-layouts  39.3 us (10%)
  between operations  16 us (4%)
    ppermute x56, waiting for transfers between devices, swap(): return lax.ppermute(value, axis, [(i, i ^ stride) for i in range(size)])  146 us
    pallas_call x41, Pallas kernels, kernel_call(): pl.pallas_call(whole, in_specs=[in_smem] * ns + [in_hbm if i in far_in el...  82.4 us
    ppermute x56, starting transfers between devices, swap(): return lax.ppermute(value, axis, [(i, i ^ stride) for i in range(size)])  63 us
    unnamed x214, local copies, waits for them, and re-layouts  30.3 us
    ppermute x6, waiting for transfers between devices, swap_slots(): lax.ppermute(value, ('dp', 'seq'), [(i, i ^ mask) for i in range(size)])  11.8 us
  transfers between devices with their start and end apart: 64, of which 32 were waited for; matrix products, arithmetic and copies ran while one was open for 2% of the time, Pallas kernels for 17%

profile of v1, /device:TPU:0, one launch (start us, length us, event | category | flops | bytes accessed | tf_op | source)
XLA Modules:
  0.0 372.1 jit_solution(3670245946246154274)
XLA Ops:
  8.8 3.1 collective-permute-start
  11.9 2.6 collective-permute-start.1
  19.4 1.6 copy-done.48
  21.0 1.6 copy-done.49
  24.5 11.8 %collective-permute-done.refs_1_.refs_4_ = bf16[256,1024]{1,0:T(8,128)(2,1)S(1)} collective-permute-done((bf16[256,1024]{1,0:T(8,128)(2,1)}, bf16[256,1024]{1,0:T(8,128)(2,1)S(1)}, u32[]{:S(2)}, u32[]{:S(2)}) %collective-permute-start) | collective-permute-done | bytes 524320 | tf_op jit(solution)/shard_map/ppermute | solution.py:35
  36.3 2.6 collective-permute-done.1.refs_0_.refs_5_
  39.8 4.2 %project.2 = (bf16[3,4,64,256]{3,2,1,0:T(8,128)(2,1)}, bf16[3,4,64,512]{3,2,1,0:T(8,128)(2,1)}) custom-call(bf16[256,1024]{1,0:T(8,128)(2,1)} %bitcast.2.refs_0_.refs_7_.refs_3_, bf16[256,1024]{1,0:T(8,128)(2,1)} %copy-done.19, bf16[256,1024]{1,0:T(8,128)(2,1)} %copy-done.50, bf16[1024,256]{1,0:T(8,128)(2,1)} %refs_3_.5, bf16[1024,256]{1,0:T(8,128)(2,1)} %refs_4_.3, ...), custom_call_target="tpu_custom_call" | custom-call | flops 1 | bytes 1 | tf_op jit(solution)/shard_map/project/pallas_call | solution.py:100
  44.0 1.6 collective-permute-start.9
  46.5 2.9 collective-permute-start.3
  49.4 12.9 %collective-permute-done.9.refs_9_.refs_16_ = bf16[3,4,64,512]{3,2,1,0:T(8,128)(2,1)} collective-permute-done((bf16[3,4,64,512]{3,2,1,0:T(8,128)(2,1)}, bf16[3,4,64,512]{3,2,1,0:T(8,128)(2,1)}, u32[]{:S(2)}, u32[]{:S(2)}) %collective-permute-start.9) | collective-permute-done | bytes 786464 | tf_op jit(solution)/shard_map/ppermute | solution.py:35
  62.3 2.9 collective-permute-done.3.refs_0_
  66.0 3.2 collective-permute-start.5
  69.3 2.9 project.3
  73.6 9.2 %collective-permute-done.5.refs_2_ = bf16[1,128,1024]{2,1,0:T(8,128)(2,1)S(1)} collective-permute-done((bf16[1,128,1024]{2,1,0:T(8,128)(2,1)S(1)}, bf16[1,128,1024]{2,1,0:T(8,128)(2,1)S(1)}, u32[]{:S(2)}, u32[]{:S(2)}) %collective-permute-start.5) | collective-permute-done | bytes 262176 | tf_op jit(solution)/shard_map/ppermute | solution.py:35
  85.4 4.5 %collective-permute-done.6.refs_3_ = bf16[1,128,1024]{2,1,0:T(8,128)(2,1)S(1)} collective-permute-done((bf16[1,128,1024]{2,1,0:T(8,128)(2,1)S(1)}, bf16[1,128,1024]{2,1,0:T(8,128)(2,1)S(1)}, u32[]{:S(2)}, u32[]{:S(2)}) %collective-permute-start.6) | collective-permute-done | bytes 262176 | tf_op jit(solution)/shard_map/ppermute | solution.py:35
  90.7 2.2 stack_pairs.1
  93.8 9.4 %attend.1 = (bf16[4,64,256]{2,1,0:T(8,128)(2,1)}, bf16[4,64,256]{2,1,0:T(8,128)(2,1)}, bf16[4,64,256]{2,1,0:T(8,128)(2,1)}, bf16[4,64,256]{2,1,0:T(8,128)(2,1)},...) custom-call(s32[6]{0:T(128)} %pad_add_fusion.refs_0_, bf16[3,4,64,256]{3,2,1,0:T(8,128)(2,1)} %get-tuple-element.106.refs_6_.refs_1_, ...), custom_call_target="tpu_custom_call" | custom-call | flops 10000000000 | bytes 1 | tf_op jit(solution)/shard_map/attend/pallas_call | solution.py:100
  103.2 1.6 collective-permute-start.14
  104.8 2.8 collective-permute-start.15
  107.6 2.6 collective-permute-start.17
  110.2 2.6 collective-permute-start.18
  112.8 2.1 collective-permute-done.14.refs_3_
  115.5 5.3 %merge_norm.1 = (f32[256,1024]{1,0:T(8,128)}, bf16[256,1024]{1,0:T(8,128)(2,1)}, f32[256,1024]{1,0:T(8,128)}, f32[256,128]{1,0:T(8,128)}, bf16[3,256,1024]{2,1,0:T(8,128)(2,1)}) custom-call(s32[1]{0:T(128)} %bitcast.refs_0_, bf16[256,256]{1,0:T(8,128)(2,1)} %bitcast.25, bf16[256,256]{1,0:T(8,128)(2,1)} %copy-done.76, bf16[256,256]{1,0:T(8,128)(2,1)} %copy-done.78, ...), custom_call_target="tpu_custom_call" | custom-call | flops 1 | bytes 1 | tf_op jit(solution)/shard_map/merge_norm/pallas_call | solution.py:100
  121.0 3.5 collective-permute-start.21
  124.5 2.1 collective-permute-start.20
  127.4 4.4 %join_units.1 = (bf16[1024,1024]{1,0:T(8,128)(2,1)}, bf16[1024,1024]{1,0:T(8,128)(2,1)}, f32[1,1024]{1,0:T(1,128)}) custom-call(bf16[4,128,1024]{2,1,0:T(8,128)(2,1)} %copy-done.7, bf16[4,128,1024]{2,1,0:T(8,128)(2,1)} %copy-done.37, bf16[4,16,128]{2,1,0:T(8,128)(2,1)} %copy-done.88, bf16[2,144,1024]{2,1,0:T(8,128)(2,1)} %get-tuple-element.110.refs_3_, ...), custom_call_target="tpu_custom_call" | custom-call | flops 1 | bytes 1 | tf_op jit(solution)/shard_map/join_units/pallas_call | solution.py:100
  131.9 1.6 copy-done
  133.5 1.6 copy-done.2
  135.7 3.6 feed_forward.2
  141.0 1.6 hold.4.refs_0_.refs_4_
  142.7 1.9 collective-permute-done.22.refs_1_.refs_5_
  144.6 2.9 feed_forward.3
  152.6 11.2 %collective-permute-done.25.refs_7_.refs_10_ = bf16[256,1024]{1,0:T(8,128)(2,1)S(1)} collective-permute-done((bf16[256,1024]{1,0:T(8,128)(2,1)S(1)}, bf16[256,1024]{1,0:T(8,128)(2,1)S(1)}, u32[]{:S(2)}, u32[]{:S(2)}) %collective-permute-start.25) | collective-permute-done | bytes 524320 | tf_op jit(solution)/shard_map/ppermute | solution.py:35
  163.8 2.9 collective-permute-done.24.refs_3_
  170.1 3.1 final_norm.1
  176.1 3.2 feed_backward.2
  180.1 8.6 %collective-permute-done.29.refs_2_.refs_11_ = bf16[256,1024]{1,0:T(8,128)(2,1)S(1)} collective-permute-done((bf16[256,1024]{1,0:T(8,128)(2,1)}, bf16[256,1024]{1,0:T(8,128)(2,1)S(1)}, u32[]{:S(2)}, u32[]{:S(2)}) %collective-permute-start.29) | collective-permute-done | bytes 524320 | tf_op jit(solution)/shard_map/ppermute | solution.py:35
  189.0 1.9 collective-permute-done.30.refs_1_.refs_5_
  191.0 2.6 feed_backward.3
  202.4 6.7 %collective-permute-done.33.refs_10_.refs_8_ = bf16[256,1024]{1,0:T(8,128)(2,1)} collective-permute-done((bf16[256,1024]{1,0:T(8,128)(2,1)}, bf16[256,1024]{1,0:T(8,128)(2,1)}, u32[]{:S(2)}, u32[]{:S(2)}) %collective-permute-start.33) | collective-permute-done | bytes 524320 | tf_op jit(solution)/shard_map/ppermute | solution.py:35
  209.2 1.5 collective-permute-done.32.refs_3_
  210.9 2.9 first_back.1
  217.5 2.8 collective-permute-start.37
  220.9 1.7 collective-permute-start.34
  222.8 16.1 %collective-permute-done.39.refs_1_ = bf16[272,1024]{1,0:T(8,128)(2,1)S(1)} collective-permute-done((bf16[272,1024]{1,0:T(8,128)(2,1)S(1)}, bf16[272,1024]{1,0:T(8,128)(2,1)S(1)}, u32[]{:S(2)}, u32[]{:S(2)}) %collective-permute-start.39) | collective-permute-done | bytes 557088 | tf_op jit(solution)/shard_map/ppermute | solution.py:35
  243.7 1.7 collective-permute-start.41
  248.2 12.6 %attend_back.1 = (bf16[4,4,64,256]{3,2,1,0:T(8,128)(2,1)}, bf16[4,4,64,512]{3,2,1,0:T(8,128)(2,1)}, bf16[4,4,64,512]{3,2,1,0:T(8,128)(2,1)}, bf16[4,4,64,512]{3,2,1,0:T(8,128)(2,1)}, bf16[4,4,64,512]{3,2,1,0:T(8,128)(2,1)}) custom-call(s32[6]{0:T(128)} %pad_add_fusion.refs_0_, bf16[3,4,64,256]{3,2,1,0:T(8,128)(2,1)} %get-tuple-element.106.refs_6_.refs_1_, ...), custom_call_target="tpu_custom_call" | custom-call | flops 20000000000 | bytes 1 | tf_op jit(solution)/shard_map/attend_back/pallas_call | solution.py:100
  265.6 4.5 %qkv_grads.1.refs_1_ = bf16[8,112,1024]{2,1,0:T(8,128)(2,1)S(1)} custom-call(s32[1]{0:T(128)} %bitcast.3.refs_0_, bf16[4,4,64,256]{3,2,1,0:T(8,128)(2,1)S(1)} %copy-done.22, bf16[4,4,64,512]{3,2,1,0:T(8,128)(2,1)S(1)} %add_split.12.refs_2_.refs_1_, bf16[256,1024]{1,0:T(8,128)(2,1)} %bitcast.2.refs_0_.refs_7_.refs_3_, bf16[256,1024]{1,0:T(8,128)(2,1)S(1)} %copy-done.21, ...), custom_call_target="tpu_custom_call" | custom-call | flops 1 | bytes 1 | tf_op jit(solution)/shard_map/qkv_grads/pallas_call | solution.py:100
  270.4 6.1 %collective-permute-start.61 = (bf16[272,1024]{1,0:T(8,128)(2,1)S(1)}, bf16[272,1024]{1,0:T(8,128)(2,1)S(1)}, u32[]{:S(2)}, u32[]{:S(2)}) collective-permute-start(bf16[272,1024]{1,0:T(8,128)(2,1)S(1)} %get-tuple-element.170.refs_12_), channel_id=1, source_target_pairs={{0,2},{1,3},{2,0},{3,1},{4,6},{5,7},{6,4},{7,5},{8,10},{9,11},{10,... | collective-permute-start | bytes 1671176 | tf_op jit(solution)/shard_map/ppermute | solution.py:35
  277.1 2.1 collective-permute-start.48
  279.2 1.5 collective-permute-start.50
  280.7 22.7 %collective-permute-done.46.refs_0_ = bf16[4,4,64,512]{3,2,1,0:T(8,128)(2,1)S(1)} collective-permute-done((bf16[4,4,64,512]{3,2,1,0:T(8,128)(2,1)S(1)}, bf16[4,4,64,512]{3,2,1,0:T(8,128)(2,1)S(1)}, u32[]{:S(2)}, u32[]{:S(2)}) %collective-permute-start.46) | collective-permute-done | bytes 1048608 | tf_op jit(solution)/shard_map/ppermute | solution.py:35
  303.4 6.5 %collective-permute-done.48.refs_1_.refs_2_ = bf16[160,1024]{1,0:T(8,128)(2,1)S(1)} collective-permute-done((bf16[160,1024]{1,0:T(8,128)(2,1)S(1)}, bf16[160,1024]{1,0:T(8,128)(2,1)S(1)}, u32[]{:S(2)}, u32[]{:S(2)}) %collective-permute-start.48) | collective-permute-done | bytes 327712 | tf_op jit(solution)/shard_map/ppermute | solution.py:40
  311.2 1.9 dtokens.1
  315.0 4.3 %collective-permute-start.52 = (bf16[256,1024]{1,0:T(8,128)(2,1)S(1)}, bf16[256,1024]{1,0:T(8,128)(2,1)S(1)}, u32[]{:S(2)}, u32[]{:S(2)}) collective-permute-start(bf16[256,1024]{1,0:T(8,128)(2,1)S(1)} %get-tuple-element.180.refs_5_.refs_2_), channel_id=1, source_target_pairs={{0,1},{1,0},{2,3},{3,2},{4,5},{5,4},{6,7},{7,6},{8,9},{9,8},{10,11... | collective-permute-start | bytes 1572872 | tf_op jit(solution)/shard_map/ppermute | solution.py:35
  320.8 2.2 collective-permute-start.56
  323.0 7.9 %collective-permute-done.52.refs_1_ = bf16[256,1024]{1,0:T(8,128)(2,1)S(1)} collective-permute-done((bf16[256,1024]{1,0:T(8,128)(2,1)S(1)}, bf16[256,1024]{1,0:T(8,128)(2,1)S(1)}, u32[]{:S(2)}, u32[]{:S(2)}) %collective-permute-start.52) | collective-permute-done | bytes 524320 | tf_op jit(solution)/shard_map/ppermute | solution.py:35
  330.9 1.7 collective-permute-start.51
  333.6 2.3 collective-permute-start.53
  335.8 5.3 %collective-permute-done.56.refs_4_ = bf16[144,1024]{1,0:T(8,128)(2,1)S(1)} collective-permute-done((bf16[144,1024]{1,0:T(8,128)(2,1)S(1)}, bf16[144,1024]{1,0:T(8,128)(2,1)S(1)}, u32[]{:S(2)}, u32[]{:S(2)}) %collective-permute-start.56) | collective-permute-done | bytes 294944 | tf_op jit(solution)/shard_map/ppermute | solution.py:40
  343.1 2.5 qkv_out.1
  346.3 8.7 %collective-permute-done.51.refs_2_ = bf16[256,1024]{1,0:T(8,128)(2,1)S(1)} collective-permute-done((bf16[256,1024]{1,0:T(8,128)(2,1)}, bf16[256,1024]{1,0:T(8,128)(2,1)S(1)}, u32[]{:S(2)}, u32[]{:S(2)}) %collective-permute-start.51) | collective-permute-done | bytes 524320 | tf_op jit(solution)/shard_map/ppermute | solution.py:35
  355.0 3.3 collective-permute-done.53.refs_3_
  360.1 4.7 %feed_out.1 = (f32[1024,1024]{1,0:T(8,128)}, f32[1024,1024]{1,0:T(8,128)}, f32[8,128]{1,0:T(8,128)}) custom-call(bf16[8,272,1024]{2,1,0:T(8,128)(2,1)} %bitcast.29), custom_call_target="tpu_custom_call" | custom-call | tf_op jit(solution)/shard_map/feed_out/pallas_call | solution.py:1028
  (346 shorter events, 69.3 us)
Async XLA Ops:
  7.2 107.7 %all-gather.5.cloned.1.call-start = ((), (), s32[]{:S(2)}) async-start(), calls=%async_computation | async-start | bytes 2162688 | tf_op jit(solution)/shard_map/all_gather | solution.py:1121
  8.7 351.4 %all-gather.7.cloned.1.call-start = ((), (), s32[]{:S(2)}) async-start(), calls=%async_computation.1 | async-start | bytes 5013504 | tf_op jit(solution)/shard_map/all_gather | solution.py:1326
  8.8 27.5 %collective-permute-start = (bf16[256,1024]{1,0:T(8,128)(2,1)}, bf16[256,1024]{1,0:T(8,128)(2,1)S(1)}, u32[]{:S(2)}, u32[]{:S(2)}) collective-permute-start(bf16[256,1024]{1,0:T(8,128)(2,1)} %bitcast.2.refs_0_.refs_7_.refs_3_), channel_id=1, source_target_pairs={{0,1},{1,0},{2,3},{3,2},{4,5},{5,4},{6,7},{7,6},{8,9},{9,8},{10,11... | collective-permute-start | bytes 1572872 | tf_op jit(solution)/shard_map/ppermute | solution.py:35
  11.9 27.0 %collective-permute-start.1 = (bf16[256,1024]{1,0:T(8,128)(2,1)}, bf16[256,1024]{1,0:T(8,128)(2,1)S(1)}, u32[]{:S(2)}, u32[]{:S(2)}) collective-permute-start(bf16[256,1024]{1,0:T(8,128)(2,1)} %bitcast.2.refs_0_.refs_7_.refs_3_), channel_id=1, source_target_pairs={{0,2},{1,3},{2,0},{3,1},{4,6},{5,7},{6,4},{7,5},{8,10},{9,11},{10,... | collective-permute-start | bytes 1572872 | tf_op jit(solution)/shard_map/ppermute | solution.py:35
  44.0 18.3 %collective-permute-start.9 = (bf16[3,4,64,512]{3,2,1,0:T(8,128)(2,1)}, bf16[3,4,64,512]{3,2,1,0:T(8,128)(2,1)}, u32[]{:S(2)}, u32[]{:S(2)}) collective-permute-start(bf16[3,4,64,512]{3,2,1,0:T(8,128)(2,1)} %get-tuple-element.112.refs_5_.refs_12_), channel_id=1, source_target_pairs={{0,8},{4,12},{8,0},{12,4},{1,9},{5,13},{9,1},{13,5},{2,10},{6,14},... | collective-permute-start | bytes 2359304 | tf_op jit(solution)/shard_map/ppermute | solution.py:35
  45.6 20.4 %collective-permute-start.2 = (bf16[256,1024]{1,0:T(8,128)(2,1)}, bf16[256,1024]{1,0:T(8,128)(2,1)}, u32[]{:S(2)}, u32[]{:S(2)}) collective-permute-start(bf16[256,1024]{1,0:T(8,128)(2,1)} %copy-done.50), channel_id=1, source_target_pairs={{0,1},{1,0},{2,3},{3,2},{4,5},{5,4},{6,7},{7,6},{8,9},{9,8},{10,11... | collective-permute-start | bytes 1572872 | tf_op jit(solution)/shard_map/ppermute | solution.py:35
  46.5 18.6 %collective-permute-start.3 = (bf16[1,144,1024]{2,1,0:T(8,128)(2,1)S(1)}, bf16[1,144,1024]{2,1,0:T(8,128)(2,1)S(1)}, u32[]{:S(2)}, u32[]{:S(2)}) collective-permute-start(bf16[1,144,1024]{2,1,0:T(8,128)(2,1)S(1)} %pack_inner.1), channel_id=1, source_target_pairs={{0,2},{1,3},{2,0},{3,1},{4,6},{5,7},{6,4},{7,5},{8,10},{9,11},{10,... | collective-permute-start | bytes 884744 | tf_op jit(solution)/shard_map/ppermute | solution.py:35
  49.4 43.5 %collective-permute-start.7 = (bf16[3,4,64,512]{3,2,1,0:T(8,128)(2,1)}, bf16[3,4,64,512]{3,2,1,0:T(8,128)(2,1)}, u32[]{:S(2)}, u32[]{:S(2)}) collective-permute-start(bf16[3,4,64,512]{3,2,1,0:T(8,128)(2,1)} %get-tuple-element.112.refs_5_.refs_12_), channel_id=1, source_target_pairs={{0,4},{4,0},{8,12},{12,8},{1,5},{5,1},{9,13},{13,9},{2,6},{6,2},{1... | collective-permute-start | bytes 2359304 | tf_op jit(solution)/shard_map/ppermute | solution.py:35
  62.3 30.7 %collective-permute-start.11 = (bf16[3,4,64,512]{3,2,1,0:T(8,128)(2,1)}, bf16[3,4,64,512]{3,2,1,0:T(8,128)(2,1)}, u32[]{:S(2)}, u32[]{:S(2)}) collective-permute-start(bf16[3,4,64,512]{3,2,1,0:T(8,128)(2,1)} %collective-permute-done.9.refs_9_.refs_16_), channel_id=1, source_target_pairs={{0,4},{4,0},{8,12},{12,8},{1,5},{5,1},{9,13},{13,9},{2,6},{6,2},{1... | collective-permute-start | bytes 2359304 | tf_op jit(solution)/shard_map/ppermute | solution.py:35
  65.2 19.2 %collective-permute-start.4 = (bf16[1,144,1024]{2,1,0:T(8,128)(2,1)S(1)}, bf16[1,144,1024]{2,1,0:T(8,128)(2,1)S(1)}, u32[]{:S(2)}, u32[]{:S(2)}) collective-permute-start(bf16[1,144,1024]{2,1,0:T(8,128)(2,1)S(1)} %collective-permute-done.3.refs_0_), channel_id=1, source_target_pairs={{0,8},{4,12},{8,0},{12,4},{1,9},{5,13},{9,1},{13,5},{2,10},{6,14},... | collective-permute-start | bytes 884744 | tf_op jit(solution)/shard_map/ppermute | solution.py:35
  66.0 16.8 %collective-permute-start.5 = (bf16[1,128,1024]{2,1,0:T(8,128)(2,1)S(1)}, bf16[1,128,1024]{2,1,0:T(8,128)(2,1)S(1)}, u32[]{:S(2)}, u32[]{:S(2)}) collective-permute-start(bf16[1,128,1024]{2,1,0:T(8,128)(2,1)S(1)} %pack_outer.1), channel_id=1, source_target_pairs={{0,2},{1,3},{2,0},{3,1},{4,6},{5,7},{6,4},{7,5},{8,10},{9,11},{10,... | collective-permute-start | bytes 786440 | tf_op jit(solution)/shard_map/ppermute | solution.py:35
  72.2 12.2 %collective-permute-start.10 = (bf16[1,4,64,512]{3,2,1,0:T(8,128)(2,1)}, bf16[1,4,64,512]{3,2,1,0:T(8,128)(2,1)S(1)}, u32[]{:S(2)}, u32[]{:S(2)}) collective-permute-start(bf16[1,4,64,512]{3,2,1,0:T(8,128)(2,1)} %get-tuple-element.113.refs_6_.refs_13_), channel_id=1, source_target_pairs={{0,8},{4,12},{8,0},{12,4},{1,9},{5,13},{9,1},{13,5},{2,10},{6,14},... | collective-permute-start | bytes 786440 | tf_op jit(solution)/shard_map/ppermute | solution.py:35
  82.8 7.1 %collective-permute-start.6 = (bf16[1,128,1024]{2,1,0:T(8,128)(2,1)S(1)}, bf16[1,128,1024]{2,1,0:T(8,128)(2,1)S(1)}, u32[]{:S(2)}, u32[]{:S(2)}) collective-permute-start(bf16[1,128,1024]{2,1,0:T(8,128)(2,1)S(1)} %collective-permute-done.5.refs_2_), channel_id=1, source_target_pairs={{0,16},{16,0},{1,17},{17,1},{2,18},{18,2},{3,19},{19,3},{4,20},{20... | collective-permute-start | bytes 786440 | tf_op jit(solution)/shard_map/ppermute | solution.py:35
  84.3 8.6 %collective-permute-start.8 = (bf16[1,4,64,512]{3,2,1,0:T(8,128)(2,1)}, bf16[1,4,64,512]{3,2,1,0:T(8,128)(2,1)S(1)}, u32[]{:S(2)}, u32[]{:S(2)}) collective-permute-start(bf16[1,4,64,512]{3,2,1,0:T(8,128)(2,1)} %get-tuple-element.113.refs_6_.refs_13_), channel_id=1, source_target_pairs={{0,4},{4,0},{8,12},{12,8},{1,5},{5,1},{9,13},{13,9},{2,6},{6,2},{1... | collective-permute-start | bytes 786440 | tf_op jit(solution)/shard_map/ppermute | solution.py:35
  84.4 8.6 %collective-permute-start.12 = (bf16[1,4,64,512]{3,2,1,0:T(8,128)(2,1)S(1)}, bf16[1,4,64,512]{3,2,1,0:T(8,128)(2,1)S(1)}, u32[]{:S(2)}, u32[]{:S(2)}) collective-permute-start(bf16[1,4,64,512]{3,2,1,0:T(8,128)(2,1)S(1)} %collective-permute-done.10.refs_10_.refs_17_), channel_id=1, source_target_pairs={{0,4},{4,0},{8,12},{12,8},{1,5},{5,1},{9,13},{13,9},{2,6},{6,2},{1... | collective-permute-start | bytes 786440 | tf_op jit(solution)/shard_map/ppermute | solution.py:35
  103.1 9.6 %collective-permute-start.13 = (bf16[256,256]{1,0:T(8,128)(2,1)}, bf16[256,256]{1,0:T(8,128)(2,1)S(1)}, u32[]{:S(2)}, u32[]{:S(2)}) collective-permute-start(bf16[256,256]{1,0:T(8,128)(2,1)} %bitcast.44), channel_id=1, source_target_pairs={{0,1},{1,0},{2,3},{3,2},{4,5},{5,4},{6,7},{7,6},{8,9},{9,8},{10,11... | collective-permute-start | bytes 393224 | tf_op jit(solution)/shard_map/ppermute | solution.py:35
  103.2 11.6 %collective-permute-start.14 = (bf16[256,256]{1,0:T(8,128)(2,1)}, bf16[256,256]{1,0:T(8,128)(2,1)S(1)}, u32[]{:S(2)}, u32[]{:S(2)}) collective-permute-start(bf16[256,256]{1,0:T(8,128)(2,1)} %bitcast.43), channel_id=1, source_target_pairs={{0,2},{1,3},{2,0},{3,1},{4,6},{5,7},{6,4},{7,5},{8,10},{9,11},{10,... | collective-permute-start | bytes 393224 | tf_op jit(solution)/shard_map/ppermute | solution.py:35
  104.8 10.0 %collective-permute-start.15 = (bf16[256,256]{1,0:T(8,128)(2,1)}, bf16[256,256]{1,0:T(8,128)(2,1)S(1)}, u32[]{:S(2)}, u32[]{:S(2)}) collective-permute-start(bf16[256,256]{1,0:T(8,128)(2,1)} %bitcast.42), channel_id=1, source_target_pairs={{0,3},{1,2},{2,1},{3,0},{4,7},{5,6},{6,5},{7,4},{8,11},{9,10},{10,... | collective-permute-start | bytes 393224 | tf_op jit(solution)/shard_map/ppermute | solution.py:35
  107.6 19.0 %collective-permute-start.17 = (bf16[2,144,1024]{2,1,0:T(8,128)(2,1)S(1)}, bf16[2,144,1024]{2,1,0:T(8,128)(2,1)S(1)}, u32[]{:S(2)}, u32[]{:S(2)}) collective-permute-start(bf16[2,144,1024]{2,1,0:T(8,128)(2,1)S(1)} %copy-done.92), channel_id=1, source_target_pairs={{0,16},{16,0},{1,17},{17,1},{2,18},{18,2},{3,19},{19,3},{4,20},{20... | collective-permute-start | bytes 1769480 | tf_op jit(solution)/shard_map/ppermute | solution.py:35
  110.2 16.4 %collective-permute-start.18 = (bf16[2,128,1024]{2,1,0:T(8,128)(2,1)}, bf16[2,128,1024]{2,1,0:T(8,128)(2,1)}, u32[]{:S(2)}, u32[]{:S(2)}) collective-permute-start(bf16[2,128,1024]{2,1,0:T(8,128)(2,1)} %get-tuple-element.111.refs_4_.refs_5_), channel_id=1, source_target_pairs={{0,8},{4,12},{8,0},{12,4},{1,9},{5,13},{9,1},{13,5},{2,10},{6,14},... | collective-permute-start | bytes 1572872 | tf_op jit(solution)/shard_map/ppermute | solution.py:35
  120.9 11.0 %collective-permute-start.16 = (bf16[256,1024]{1,0:T(8,128)(2,1)}, bf16[256,1024]{1,0:T(8,128)(2,1)S(1)}, u32[]{:S(2)}, u32[]{:S(2)}) collective-permute-start(bf16[256,1024]{1,0:T(8,128)(2,1)} %get-tuple-element.119.refs_7_.refs_0_.refs_2_), channel_id=1, source_target_pairs={{0,4},{4,0},{8,12},{12,8},{1,5},{5,1},{9,13},{13,9},{2,6},{6,2},{1... | collective-permute-start | bytes 1572872 | tf_op jit(solution)/shard_map/ppermute | solution.py:35
  121.0 20.0 %collective-permute-start.21 = (bf16[256,1024]{1,0:T(8,128)(2,1)S(1)}, bf16[256,1024]{1,0:T(8,128)(2,1)}, u32[]{:S(2)}, u32[]{:S(2)}) collective-permute-start(bf16[256,1024]{1,0:T(8,128)(2,1)S(1)} %copy-done.20), channel_id=1, source_target_pairs={{0,8},{4,12},{8,0},{12,4},{1,9},{5,13},{9,1},{13,5},{2,10},{6,14},... | collective-permute-start | bytes 1572872 | tf_op jit(solution)/shard_map/ppermute | solution.py:35
  124.5 16.5 %collective-permute-start.20 = (bf16[256,1024]{1,0:T(8,128)(2,1)}, bf16[256,1024]{1,0:T(8,128)(2,1)}, u32[]{:S(2)}, u32[]{:S(2)}) collective-permute-start(bf16[256,1024]{1,0:T(8,128)(2,1)} %get-tuple-element.119.refs_7_.refs_0_.refs_2_), channel_id=1, source_target_pairs={{0,1},{1,0},{2,3},{3,2},{4,5},{5,4},{6,7},{7,6},{8,9},{9,8},{10,11... | collective-permute-start | bytes 1572872 | tf_op jit(solution)/shard_map/ppermute | solution.py:35
  142.6 2.0 collective-permute-start.22
  149.5 1.9 collective-permute-start.23
  149.6 14.2 %collective-permute-start.25 = (bf16[256,1024]{1,0:T(8,128)(2,1)S(1)}, bf16[256,1024]{1,0:T(8,128)(2,1)S(1)}, u32[]{:S(2)}, u32[]{:S(2)}) collective-permute-start(bf16[256,1024]{1,0:T(8,128)(2,1)S(1)} %collective-permute-done.1.refs_0_.refs_5_), channel_id=1, source_target_pairs={{0,8},{4,12},{8,0},{12,4},{1,9},{5,13},{9,1},{13,5},{2,10},{6,14},... | collective-permute-start | bytes 1572872 | tf_op jit(solution)/shard_map/ppermute | solution.py:35
  149.7 14.1 %collective-permute-start.19 = (bf16[256,1024]{1,0:T(8,128)(2,1)}, bf16[256,1024]{1,0:T(8,128)(2,1)}, u32[]{:S(2)}, u32[]{:S(2)}) collective-permute-start(bf16[256,1024]{1,0:T(8,128)(2,1)} %get-tuple-element.124), channel_id=1, source_target_pairs={{0,4},{4,0},{8,12},{12,8},{1,5},{5,1},{9,13},{13,9},{2,6},{6,2},{1... | collective-permute-start | bytes 1572872 | tf_op jit(solution)/shard_map/ppermute | solution.py:35
  152.3 14.3 %collective-permute-start.24 = (bf16[256,1024]{1,0:T(8,128)(2,1)}, bf16[256,1024]{1,0:T(8,128)(2,1)}, u32[]{:S(2)}, u32[]{:S(2)}) collective-permute-start(bf16[256,1024]{1,0:T(8,128)(2,1)} %add_split.8), channel_id=1, source_target_pairs={{0,1},{1,0},{2,3},{3,2},{4,5},{5,4},{6,7},{7,6},{8,9},{9,8},{10,11... | collective-permute-start | bytes 1572872 | tf_op jit(solution)/shard_map/ppermute | solution.py:35
  174.2 1.9 collective-permute-start.26
  174.2 14.5 %collective-permute-start.29 = (bf16[256,1024]{1,0:T(8,128)(2,1)}, bf16[256,1024]{1,0:T(8,128)(2,1)S(1)}, u32[]{:S(2)}, u32[]{:S(2)}) collective-permute-start(bf16[256,1024]{1,0:T(8,128)(2,1)} %collective-permute-done.2.refs_0_.refs_1_.refs_6_), channel_id=1, source_target_pairs={{0,8},{4,12},{8,0},{12,4},{1,9},{5,13},{9,1},{13,5},{2,10},{6,14},... | collective-permute-start | bytes 1572872 | tf_op jit(solution)/shard_map/ppermute | solution.py:35
  174.9 14.1 %collective-permute-start.28 = (bf16[256,1024]{1,0:T(8,128)(2,1)S(1)}, bf16[256,1024]{1,0:T(8,128)(2,1)S(1)}, u32[]{:S(2)}, u32[]{:S(2)}) collective-permute-start(bf16[256,1024]{1,0:T(8,128)(2,1)S(1)} %get-tuple-element.130.refs_0_.refs_2_), channel_id=1, source_target_pairs={{0,1},{1,0},{2,3},{3,2},{4,5},{5,4},{6,7},{7,6},{8,9},{9,8},{10,11... | collective-permute-start | bytes 1572872 | tf_op jit(solution)/shard_map/ppermute | solution.py:35
  189.0 2.0 collective-permute-start.30
  194.5 1.9 collective-permute-start.31
  194.7 14.5 %collective-permute-start.33 = (bf16[256,1024]{1,0:T(8,128)(2,1)}, bf16[256,1024]{1,0:T(8,128)(2,1)}, u32[]{:S(2)}, u32[]{:S(2)}) collective-permute-start(bf16[256,1024]{1,0:T(8,128)(2,1)} %bitcast.2.refs_0_.refs_7_.refs_3_), channel_id=1, source_target_pairs={{0,8},{4,12},{8,0},{12,4},{1,9},{5,13},{9,1},{13,5},{2,10},{6,14},... | collective-permute-start | bytes 1572872 | tf_op jit(solution)/shard_map/ppermute | solution.py:35
  196.0 13.1 %collective-permute-start.27 = (bf16[256,1024]{1,0:T(8,128)(2,1)}, bf16[256,1024]{1,0:T(8,128)(2,1)}, u32[]{:S(2)}, u32[]{:S(2)}) collective-permute-start(bf16[256,1024]{1,0:T(8,128)(2,1)} %get-tuple-element.133), channel_id=1, source_target_pairs={{0,4},{4,0},{8,12},{12,8},{1,5},{5,1},{9,13},{13,9},{2,6},{6,2},{1... | collective-permute-start | bytes 1572872 | tf_op jit(solution)/shard_map/ppermute | solution.py:35
  196.6 14.1 %collective-permute-start.32 = (bf16[256,1024]{1,0:T(8,128)(2,1)S(1)}, bf16[256,1024]{1,0:T(8,128)(2,1)}, u32[]{:S(2)}, u32[]{:S(2)}) collective-permute-start(bf16[256,1024]{1,0:T(8,128)(2,1)S(1)} %add_split.9.refs_6_), channel_id=1, source_target_pairs={{0,1},{1,0},{2,3},{3,2},{4,5},{5,4},{6,7},{7,6},{8,9},{9,8},{10,11... | collective-permute-start | bytes 1572872 | tf_op jit(solution)/shard_map/ppermute | solution.py:35
  214.7 5.5 %collective-permute-start.38 = (bf16[528,1024]{1,0:T(8,128)(2,1)S(1)}, bf16[528,1024]{1,0:T(8,128)(2,1)S(1)}, u32[]{:S(2)}, u32[]{:S(2)}) collective-permute-start(bf16[528,1024]{1,0:T(8,128)(2,1)S(1)} %get-tuple-element.154), channel_id=1, source_target_pairs={{0,4},{4,0},{8,12},{12,8},{1,5},{5,1},{9,13},{13,9},{2,6},{6,2},{1... | collective-permute-start | bytes 3244040 | tf_op jit(solution)/shard_map/ppermute | solution.py:35
  214.7 28.4 %collective-permute-start.40 = (bf16[2,272,1024]{2,1,0:T(8,128)(2,1)S(1)}, bf16[2,272,1024]{2,1,0:T(8,128)(2,1)S(1)}, u32[]{:S(2)}, u32[]{:S(2)}) collective-permute-start(bf16[2,272,1024]{2,1,0:T(8,128)(2,1)S(1)} %weight_grad.4.refs_9_), channel_id=1, source_target_pairs={{0,8},{4,12},{8,0},{12,4},{1,9},{5,13},{9,1},{13,5},{2,10},{6,14},... | collective-permute-start | bytes 3342344 | tf_op jit(solution)/shard_map/ppermute | solution.py:35
  217.5 26.2 %collective-permute-start.37 = (bf16[2,256,1024]{2,1,0:T(8,128)(2,1)S(1)}, bf16[2,256,1024]{2,1,0:T(8,128)(2,1)S(1)}, u32[]{:S(2)}, u32[]{:S(2)}) collective-permute-start(bf16[2,256,1024]{2,1,0:T(8,128)(2,1)S(1)} %weight_grad.6), channel_id=1, source_target_pairs={{0,16},{16,0},{1,17},{17,1},{2,18},{18,2},{3,19},{19,3},{4,20},{20... | collective-permute-start | bytes 3145736 | tf_op jit(solution)/shard_map/ppermute | solution.py:35
  220.5 18.4 %collective-permute-start.39 = (bf16[272,1024]{1,0:T(8,128)(2,1)S(1)}, bf16[272,1024]{1,0:T(8,128)(2,1)S(1)}, u32[]{:S(2)}, u32[]{:S(2)}) collective-permute-start(bf16[272,1024]{1,0:T(8,128)(2,1)S(1)} %get-tuple-element.156), channel_id=1, source_target_pairs={{0,1},{1,0},{2,3},{3,2},{4,5},{5,4},{6,7},{7,6},{8,9},{9,8},{10,11... | collective-permute-start | bytes 1671176 | tf_op jit(solution)/shard_map/ppermute | solution.py:35
  220.9 25.7 %collective-permute-start.34 = (bf16[256,256]{1,0:T(8,128)(2,1)S(1)}, bf16[256,256]{1,0:T(8,128)(2,1)S(1)}, u32[]{:S(2)}, u32[]{:S(2)}) collective-permute-start(bf16[256,256]{1,0:T(8,128)(2,1)S(1)} %get-tuple-element.144), channel_id=1, source_target_pairs={{0,1},{1,0},{2,3},{3,2},{4,5},{5,4},{6,7},{7,6},{8,9},{9,8},{10,11... | collective-permute-start | bytes 393224 | tf_op jit(solution)/shard_map/ppermute | solution.py:35
  222.6 24.9 %collective-permute-start.35 = (bf16[256,256]{1,0:T(8,128)(2,1)S(1)}, bf16[256,256]{1,0:T(8,128)(2,1)S(1)}, u32[]{:S(2)}, u32[]{:S(2)}) collective-permute-start(bf16[256,256]{1,0:T(8,128)(2,1)S(1)} %get-tuple-element.145), channel_id=1, source_target_pairs={{0,2},{1,3},{2,0},{3,1},{4,6},{5,7},{6,4},{7,5},{8,10},{9,11},{10,... | collective-permute-start | bytes 393224 | tf_op jit(solution)/shard_map/ppermute | solution.py:35
  238.9 8.6 %collective-permute-start.36 = (bf16[256,256]{1,0:T(8,128)(2,1)S(1)}, bf16[256,256]{1,0:T(8,128)(2,1)S(1)}, u32[]{:S(2)}, u32[]{:S(2)}) collective-permute-start(bf16[256,256]{1,0:T(8,128)(2,1)S(1)} %get-tuple-element.146), channel_id=1, source_target_pairs={{0,3},{1,2},{2,1},{3,0},{4,7},{5,6},{6,5},{7,4},{8,11},{9,10},{10,... | collective-permute-start | bytes 393224 | tf_op jit(solution)/shard_map/ppermute | solution.py:35
  243.2 17.6 %collective-permute-start.43 = (bf16[144,1024]{1,0:T(8,128)(2,1)S(1)}, bf16[144,1024]{1,0:T(8,128)(2,1)S(1)}, u32[]{:S(2)}, u32[]{:S(2)}) collective-permute-start(bf16[144,1024]{1,0:T(8,128)(2,1)S(1)} %get-tuple-element.158.refs_2_.refs_11_), channel_id=1, source_target_pairs={{0,2},{1,3},{2,0},{3,1},{4,6},{5,7},{6,4},{7,5},{8,10},{9,11},{10,... | collective-permute-start | bytes 884744 | tf_op jit(solution)/shard_map/ppermute | solution.py:35
  243.7 17.1 %collective-permute-start.41 = (bf16[1,272,1024]{2,1,0:T(8,128)(2,1)S(1)}, bf16[1,272,1024]{2,1,0:T(8,128)(2,1)S(1)}, u32[]{:S(2)}, u32[]{:S(2)}) collective-permute-start(bf16[1,272,1024]{2,1,0:T(8,128)(2,1)S(1)} %get-tuple-element.165), channel_id=1, source_target_pairs={{0,16},{16,0},{1,17},{17,1},{2,18},{18,2},{3,19},{19,3},{4,20},{20... | collective-permute-start | bytes 1671176 | tf_op jit(solution)/shard_map/ppermute | solution.py:35
  246.6 14.2 %collective-permute-start.42 = (bf16[1,256,1024]{2,1,0:T(8,128)(2,1)S(1)}, bf16[1,256,1024]{2,1,0:T(8,128)(2,1)S(1)}, u32[]{:S(2)}, u32[]{:S(2)}) collective-permute-start(bf16[1,256,1024]{2,1,0:T(8,128)(2,1)S(1)} %get-tuple-element.166), channel_id=1, source_target_pairs={{0,8},{4,12},{8,0},{12,4},{1,9},{5,13},{9,1},{13,5},{2,10},{6,14},... | collective-permute-start | bytes 1572872 | tf_op jit(solution)/shard_map/ppermute | solution.py:35
  260.8 2.9 collective-permute-start.44
  260.9 4.4 %collective-permute-start.45 = (bf16[4,4,64,512]{3,2,1,0:T(8,128)(2,1)}, bf16[4,4,64,512]{3,2,1,0:T(8,128)(2,1)S(1)}, u32[]{:S(2)}, u32[]{:S(2)}) collective-permute-start(bf16[4,4,64,512]{3,2,1,0:T(8,128)(2,1)} %get-tuple-element.169), channel_id=1, source_target_pairs={{0,4},{4,0},{8,12},{12,8},{1,5},{5,1},{9,13},{13,9},{2,6},{6,2},{1... | collective-permute-start | bytes 3145736 | tf_op jit(solution)/shard_map/ppermute | solution.py:35
  270.2 6.3 %collective-permute-start.47 = (bf16[4,112,1024]{2,1,0:T(8,128)(2,1)S(1)}, bf16[4,112,1024]{2,1,0:T(8,128)(2,1)S(1)}, u32[]{:S(2)}, u32[]{:S(2)}) collective-permute-start(bf16[4,112,1024]{2,1,0:T(8,128)(2,1)S(1)} %slice.40), channel_id=1, source_target_pairs={{0,4},{4,0},{8,12},{12,8},{1,5},{5,1},{9,13},{13,9},{2,6},{6,2},{1... | collective-permute-start | bytes 2752520 | tf_op jit(solution)/shard_map/ppermute | solution.py:35
  270.4 33.0 %collective-permute-start.46 = (bf16[4,4,64,512]{3,2,1,0:T(8,128)(2,1)S(1)}, bf16[4,4,64,512]{3,2,1,0:T(8,128)(2,1)S(1)}, u32[]{:S(2)}, u32[]{:S(2)}) collective-permute-start(bf16[4,4,64,512]{3,2,1,0:T(8,128)(2,1)S(1)} %add_split.13.refs_7_), channel_id=1, source_target_pairs={{0,8},{4,12},{8,0},{12,4},{1,9},{5,13},{9,1},{13,5},{2,10},{6,14},... | collective-permute-start | bytes 3145736 | tf_op jit(solution)/shard_map/ppermute | solution.py:35
  270.4 43.6 %collective-permute-start.61 = (bf16[272,1024]{1,0:T(8,128)(2,1)S(1)}, bf16[272,1024]{1,0:T(8,128)(2,1)S(1)}, u32[]{:S(2)}, u32[]{:S(2)}) collective-permute-start(bf16[272,1024]{1,0:T(8,128)(2,1)S(1)} %get-tuple-element.170.refs_12_), channel_id=1, source_target_pairs={{0,2},{1,3},{2,0},{3,1},{4,6},{5,7},{6,4},{7,5},{8,10},{9,11},{10,... | collective-permute-start | bytes 1671176 | tf_op jit(solution)/shard_map/ppermute | solution.py:35
  277.1 32.8 %collective-permute-start.48 = (bf16[160,1024]{1,0:T(8,128)(2,1)S(1)}, bf16[160,1024]{1,0:T(8,128)(2,1)S(1)}, u32[]{:S(2)}, u32[]{:S(2)}) collective-permute-start(bf16[160,1024]{1,0:T(8,128)(2,1)S(1)} %get-tuple-element.173), channel_id=1, source_target_pairs={{0,8},{4,12},{8,0},{12,4},{16,24},{20,28},{24,16},{28,20},{1,9},{5... | collective-permute-start | bytes 983048 | tf_op jit(solution)/shard_map/ppermute | solution.py:40
  279.2 30.7 %collective-permute-start.49 = (bf16[160,1024]{1,0:T(8,128)(2,1)S(1)}, bf16[160,1024]{1,0:T(8,128)(2,1)S(1)}, u32[]{:S(2)}, u32[]{:S(2)}) collective-permute-start(bf16[160,1024]{1,0:T(8,128)(2,1)S(1)} %get-tuple-element.174), channel_id=1, source_target_pairs={{0,16},{4,20},{8,24},{12,28},{16,0},{20,4},{24,8},{28,12},{1,17},{... | collective-permute-start | bytes 983048 | tf_op jit(solution)/shard_map/ppermute | solution.py:40
  279.2 30.7 %collective-permute-start.50 = (bf16[160,1024]{1,0:T(8,128)(2,1)S(1)}, bf16[160,1024]{1,0:T(8,128)(2,1)S(1)}, u32[]{:S(2)}, u32[]{:S(2)}) collective-permute-start(bf16[160,1024]{1,0:T(8,128)(2,1)S(1)} %get-tuple-element.175), channel_id=1, source_target_pairs={{0,24},{4,28},{8,16},{12,20},{16,8},{20,12},{24,0},{28,4},{1,25},{... | collective-permute-start | bytes 983048 | tf_op jit(solution)/shard_map/ppermute | solution.py:40
  315.0 15.9 %collective-permute-start.52 = (bf16[256,1024]{1,0:T(8,128)(2,1)S(1)}, bf16[256,1024]{1,0:T(8,128)(2,1)S(1)}, u32[]{:S(2)}, u32[]{:S(2)}) collective-permute-start(bf16[256,1024]{1,0:T(8,128)(2,1)S(1)} %get-tuple-element.180.refs_5_.refs_2_), channel_id=1, source_target_pairs={{0,1},{1,0},{2,3},{3,2},{4,5},{5,4},{6,7},{7,6},{8,9},{9,8},{10,11... | collective-permute-start | bytes 1572872 | tf_op jit(solution)/shard_map/ppermute | solution.py:35
  319.4 14.1 %collective-permute-start.54 = (bf16[144,1024]{1,0:T(8,128)(2,1)S(1)}, bf16[144,1024]{1,0:T(8,128)(2,1)S(1)}, u32[]{:S(2)}, u32[]{:S(2)}) collective-permute-start(bf16[144,1024]{1,0:T(8,128)(2,1)S(1)} %get-tuple-element.182.refs_2_.refs_1_), channel_id=1, source_target_pairs={{0,8},{4,12},{8,0},{12,4},{16,24},{20,28},{24,16},{28,20},{1,9},{5... | collective-permute-start | bytes 884744 | tf_op jit(solution)/shard_map/ppermute | solution.py:40
  319.8 16.1 %collective-permute-start.55 = (bf16[144,1024]{1,0:T(8,128)(2,1)S(1)}, bf16[144,1024]{1,0:T(8,128)(2,1)S(1)}, u32[]{:S(2)}, u32[]{:S(2)}) collective-permute-start(bf16[144,1024]{1,0:T(8,128)(2,1)S(1)} %get-tuple-element.182.refs_2_.refs_1_), channel_id=1, source_target_pairs={{0,16},{4,20},{8,24},{12,28},{16,0},{20,4},{24,8},{28,12},{1,17},{... | collective-permute-start | bytes 884744 | tf_op jit(solution)/shard_map/ppermute | solution.py:40
  320.8 20.4 %collective-permute-start.56 = (bf16[144,1024]{1,0:T(8,128)(2,1)S(1)}, bf16[144,1024]{1,0:T(8,128)(2,1)S(1)}, u32[]{:S(2)}, u32[]{:S(2)}) collective-permute-start(bf16[144,1024]{1,0:T(8,128)(2,1)S(1)} %get-tuple-element.182.refs_2_.refs_1_), channel_id=1, source_target_pairs={{0,24},{4,28},{8,16},{12,20},{16,8},{20,12},{24,0},{28,4},{1,25},{... | collective-permute-start | bytes 884744 | tf_op jit(solution)/shard_map/ppermute | solution.py:40
  323.0 18.2 %collective-permute-start.57 = (bf16[144,1024]{1,0:T(8,128)(2,1)S(1)}, bf16[144,1024]{1,0:T(8,128)(2,1)S(1)}, u32[]{:S(2)}, u32[]{:S(2)}) collective-permute-start(bf16[144,1024]{1,0:T(8,128)(2,1)S(1)} %get-tuple-element.182.refs_2_.refs_1_), channel_id=1, source_target_pairs={{0,4},{4,0},{8,12},{12,8},{1,5},{5,1},{9,13},{13,9},{2,6},{6,2},{1... | collective-permute-start | bytes 884744 | tf_op jit(solution)/shard_map/ppermute | solution.py:35
  330.9 24.1 %collective-permute-start.51 = (bf16[256,1024]{1,0:T(8,128)(2,1)}, bf16[256,1024]{1,0:T(8,128)(2,1)S(1)}, u32[]{:S(2)}, u32[]{:S(2)}) collective-permute-start(bf16[256,1024]{1,0:T(8,128)(2,1)} %get-tuple-element.178), channel_id=1, source_target_pairs={{0,1},{1,0},{2,3},{3,2},{4,5},{5,4},{6,7},{7,6},{8,9},{9,8},{10,11... | collective-permute-start | bytes 1572872 | tf_op jit(solution)/shard_map/ppermute | solution.py:35
  333.6 24.8 %collective-permute-start.53 = (bf16[256,1024]{1,0:T(8,128)(2,1)}, bf16[256,1024]{1,0:T(8,128)(2,1)S(1)}, u32[]{:S(2)}, u32[]{:S(2)}) collective-permute-start(bf16[256,1024]{1,0:T(8,128)(2,1)} %add_split.14), channel_id=1, source_target_pairs={{0,2},{1,3},{2,0},{3,1},{4,6},{5,7},{6,4},{7,5},{8,10},{9,11},{10,... | collective-permute-start | bytes 1572872 | tf_op jit(solution)/shard_map/ppermute | solution.py:35
  335.8 6.4 %collective-permute-start.58 = (bf16[144,1024]{1,0:T(8,128)(2,1)S(1)}, bf16[144,1024]{1,0:T(8,128)(2,1)S(1)}, u32[]{:S(2)}, u32[]{:S(2)}) collective-permute-start(bf16[144,1024]{1,0:T(8,128)(2,1)S(1)} %collective-permute-done.54.refs_2_), channel_id=1, source_target_pairs={{0,4},{4,0},{8,12},{12,8},{1,5},{5,1},{9,13},{13,9},{2,6},{6,2},{1... | collective-permute-start | bytes 884744 | tf_op jit(solution)/shard_map/ppermute | solution.py:35
  341.1 1.6 collective-permute-start.59
  341.1 2.0 collective-permute-start.60
  (107 other events, 730.1 us)
Sparse Core Ops, SparseCore 0:
  11.6 76.7 all-gather.4
  315.1 45.0 all-gather.6
